TPU v7x, 32 devices: a whole 2x2x4 slice. The times are simulated.
32 devices in a mesh: seq: 8 (over z, y), head: 4 (over x, core).
Axes of the slice: x: 2, y: 2, z: 4, core: 2. Of those that a mesh axis runs over, the one named last changes fastest.
Arguments:
- inputs: bfloat16 [8192, 1024], P('seq', 'head'), may hold values from -6 to 6
- cotangent: bfloat16 [8192, 1024], P('seq', 'head'), may hold values from -6 to 6
- norm_gain: bfloat16 [1024], P('head'), may hold values from 0.5 to 1.5
- qkv_weight: bfloat16 [3, 1024, 1024], P(None, None, 'head'), may hold values from -0.25 to 0.25
- conv_kernel: float32 [4, 3, 1024], P(None, None, 'head'), may hold values from -3 to 3
- persistent: bfloat16 [2, 16, 1024], P(None, None, 'head'), may hold values from -8 to 8
- out_weight: bfloat16 [1024, 1024], P('head'), may hold values from -0.1875 to 0.1875
- ffn_gain: bfloat16 [1024], P('head'), may hold values from 0.5 to 1.5
- gate_up: bfloat16 [2, 1024, 2816], P(None, None, 'head'), may hold values from -0.1875 to 0.1875
- down_weight: bfloat16 [2816, 1024], P('head'), may hold values from -0.109375 to 0.109375
- memory_decay: float32 [8192, 8], P('seq', 'head'), may hold values from 0.5 to 1
- momentum_decay: float32 [8192, 8], P('seq', 'head'), may hold values from 0.5 to 1
- doc_start: int32 [8192], P('seq'), may hold values from 0 to 8191, as said below
Outputs:
- output: bfloat16 [8192, 1024], P('seq', 'head')
- input_grad: float32 [8192, 1024], P('seq', 'head')
- grad_norm_gain: float32 [1024], P('head')
- grad_qkv: float32 [3, 1024, 1024], P(None, 'seq', 'head')
- grad_conv: float32 [4, 3, 1024], P(None, None, 'head')
- grad_persistent: float32 [2, 16, 1024], P(None, None, 'head')
- grad_out: float32 [1024, 1024], P('head', 'seq')
- grad_ffn_gain: float32 [1024], P('head')
- grad_gate_up: float32 [2, 1024, 2816], P(None, 'seq', 'head')
- grad_down: float32 [2816, 1024], P('head', 'seq')
Inputs may be any that keep to these rules, and one draw needn't show every extreme that they name: doc_start[t] <= t, and doc_start[t] is t or doc_start[t - 1].
All inputs are finite; a program needn't handle non-finite values.
Results may differ from a plain program's by a relative error of at most 0.02.
Values may be sent and summed in bfloat16 or wider, within the bound.
No kernel may reach another device: no remote copies, remote signals or barrier semaphores. Data moves between devices by JAX's collectives and lax.ppermute only.
A program may use at most 192 MiB of HBM per device.

v0:
```python
import jax
import jax.numpy as jnp
from jax import lax
from jax.sharding import PartitionSpec as P

DH = 128
KW = 4
SEG = 1024
QBLK = 512
MBLK = 256


MEMORY_PRECISION = lax.Precision.HIGH
EPSILON = 1e-06
MEMORY_FLOOR = 64.0
MASKED = -1e30


def from_behind(shard, axis, by):
    peers = lax.axis_size(axis)
    pairs = [(i, i + by) for i in range(peers) if 0 <= i + by < peers]
    return lax.ppermute(shard, axis, pairs)


def entering(shard, axis, join, neutral, backward):
    count = lax.axis_size(axis)
    place = lax.axis_index(axis)
    ahead = count - 1 - place if backward else place
    gathered = jax.tree.map(
        lambda a, kind: lax.all_gather(a.astype(kind), axis),
        shard,
        jax.tree.map(lambda a: jnp.bfloat16 if a.dtype == jnp.float32 else a.dtype, shard),
    )
    state = jax.tree.map(lambda a, e: jnp.zeros_like(a) + jnp.asarray(e, a.dtype), shard, neutral)

    def one(lap, state):
        source = count - 1 - lap if backward else lap
        return join(
            state,
            jax.tree.map(
                lambda a, own: lax.dynamic_index_in_dim(a, source, 0, False).astype(own.dtype),
                gathered,
                shard,
            ),
        )

    return lax.fori_loop(0, ahead, one, state)


def memory_block(
    carry_mem, carry_mom, query_block, key_block, value_block, log_keep, log_carry, starts, places
):
    keep_sum = jnp.cumsum(log_keep)
    carry_sum = jnp.cumsum(log_carry)
    linked = (starts[:, None] <= places[None, :]) & (places[None, :] <= places[:, None])
    keep_mat = jnp.where(
        linked, jnp.exp(jnp.minimum(keep_sum[:, None] - keep_sum[None, :], 0.0)), 0.0
    )
    carry_mat = jnp.where(
        linked, jnp.exp(jnp.minimum(carry_sum[:, None] - carry_sum[None, :], 0.0)), 0.0
    )
    fresh_rows = starts < places[0]
    keep_weight = jnp.where(fresh_rows, jnp.exp(keep_sum), 0.0)
    carried = jnp.where(fresh_rows, jnp.exp(carry_sum), 0.0)
    kernel = jnp.dot(keep_mat, carry_mat, precision=MEMORY_PRECISION)
    cross_weight = jnp.dot(keep_mat, carried, precision=MEMORY_PRECISION)
    affinity = jnp.dot(query_block, key_block.T, precision=MEMORY_PRECISION)
    reading = jnp.dot(kernel * affinity, value_block, precision=MEMORY_PRECISION)
    reading = reading + keep_weight[:, None] * jnp.dot(
        query_block, carry_mem.T, precision=MEMORY_PRECISION
    )
    reading = reading + cross_weight[:, None] * jnp.dot(
        query_block, carry_mom.T, precision=MEMORY_PRECISION
    )
    mem_end = (
        keep_weight[-1] * carry_mem
        + cross_weight[-1] * carry_mom
        + jnp.dot((value_block * kernel[-1][:, None]).T, key_block, precision=MEMORY_PRECISION)
    )
    mom_end = carried[-1] * carry_mom + jnp.dot(
        (value_block * carry_mat[-1][:, None]).T, key_block, precision=MEMORY_PRECISION
    )
    return (reading, mem_end, mom_end, keep_weight, cross_weight, carried)


def compose(earlier_map, later_map):
    keep_one, cross_one, carry_one, mem_one, mom_one = earlier_map
    keep_two, cross_two, carry_two, mem_two, mom_two = later_map
    return (
        keep_two * keep_one,
        keep_two * cross_one + cross_two * carry_one,
        carry_two * carry_one,
        keep_two[:, None, None] * mem_one + cross_two[:, None, None] * mom_one + mem_two,
        carry_two[:, None, None] * mom_one + mom_two,
    )


def pull_back(earlier_map, later_map):
    keep_high, cross_high, carry_high, mem_high, mom_high = earlier_map
    keep_low, cross_low, carry_low, mem_low, mom_low = later_map
    return (
        keep_high * keep_low,
        keep_high * cross_low + cross_high * carry_low,
        carry_high * carry_low,
        mem_low + keep_low[:, None, None] * mem_high,
        mom_low + cross_low[:, None, None] * mem_high + carry_low[:, None, None] * mom_high,
    )


def memory_local(queries, key_rows, value_rows, log_keep, log_carry, starts, places):
    row_count, head_count, head_width = queries.shape
    block_count = row_count // MBLK

    def blocks(tensor):
        return tensor.reshape(block_count, MBLK, head_count, head_width).transpose(0, 2, 1, 3)

    def rate_blocks(tensor):
        return tensor.reshape(block_count, MBLK, head_count).transpose(0, 2, 1)

    def advance(carry, pieces):
        memory, momentum, keep_dev, cross_dev, carry_dev = carry
        reading, mem_end, mom_end, keep_weight, cross_weight, carried = jax.vmap(
            memory_block, in_axes=(0, 0, 0, 0, 0, 0, 0, None, None)
        )(memory, momentum, *pieces)
        keep_rows = keep_weight * keep_dev[:, None]
        cross_rows = keep_weight * cross_dev[:, None] + cross_weight * carry_dev[:, None]
        new_state = (
            mem_end,
            mom_end,
            keep_weight[:, -1] * keep_dev,
            keep_weight[:, -1] * cross_dev + cross_weight[:, -1] * carry_dev,
            carried[:, -1] * carry_dev,
        )
        return (new_state, (reading, keep_rows, cross_rows))

    zero_state = jnp.zeros((head_count, head_width, head_width), jnp.float32)
    ones_head = jnp.ones((head_count,), jnp.float32)
    zeros_head = jnp.zeros((head_count,), jnp.float32)
    scanned = (
        blocks(queries),
        blocks(key_rows),
        blocks(value_rows),
        rate_blocks(log_keep),
        rate_blocks(log_carry),
        starts.reshape(block_count, MBLK),
        places.reshape(block_count, MBLK),
    )
    final, (readings, keep_all, cross_all) = lax.scan(
        jax.checkpoint(advance), (zero_state, zero_state, ones_head, zeros_head, ones_head), scanned
    )
    reading = readings.transpose(0, 2, 1, 3).reshape(row_count, head_count, head_width)
    keep_rows = keep_all.transpose(0, 2, 1).reshape(row_count, head_count)
    cross_rows = cross_all.transpose(0, 2, 1).reshape(row_count, head_count)
    return ((reading, final[0], final[1]), (keep_rows, cross_rows, final[2], final[3], final[4]))


def correction(queries, memory_in, momentum_in, keep_rows, cross_rows):
    from_memory = jnp.einsum("thd,hed->the", queries, memory_in, precision=MEMORY_PRECISION)
    from_momentum = jnp.einsum("thd,hed->the", queries, momentum_in, precision=MEMORY_PRECISION)
    return keep_rows[:, :, None] * from_memory + cross_rows[:, :, None] * from_momentum


def score_block(queries, query_rows, starts, all_keys, offset, fixed_count):
    row_count = all_keys.shape[0] - fixed_count
    raw_scores = jnp.einsum("bhd,khd->hbk", queries, all_keys, preferred_element_type=jnp.float32)
    key_index = jnp.arange(fixed_count + row_count, dtype=jnp.int32) - fixed_count
    same_seg = key_index[None, :] // SEG == query_rows[:, None] // SEG
    token_ok = (
        same_seg
        & (key_index[None, :] <= query_rows[:, None])
        & (offset + key_index[None, :] >= starts[:, None])
    )
    visible = (key_index[None, :] < 0) | token_ok
    return jnp.where(visible[None], raw_scores * queries.shape[-1] ** (-0.5), MASKED)


def attend_forward(queries, query_rows, starts, all_keys, all_values, offset, fixed_count):
    scores = score_block(queries, query_rows, starts, all_keys, offset, fixed_count)
    row_top = jnp.max(scores, -1, keepdims=True)
    log_total = row_top + jnp.log(jnp.sum(jnp.exp(scores - row_top), -1, keepdims=True))
    weights = jnp.exp(scores - log_total).astype(jnp.bfloat16)
    return (
        jnp.einsum("hbk,khd->bhd", weights, all_values, preferred_element_type=jnp.float32),
        log_total,
    )


def attend_backward(
    queries, query_rows, starts, all_keys, all_values, offset, fixed_count, log_total, grad_rows
):
    scores = score_block(queries, query_rows, starts, all_keys, offset, fixed_count)
    weights = jnp.exp(scores - log_total)
    weights_low = weights.astype(jnp.bfloat16)
    grad_weights = jnp.einsum(
        "bhd,khd->hbk", grad_rows, all_values, preferred_element_type=jnp.float32
    )
    grad_values = jnp.einsum(
        "hbk,bhd->khd", weights_low, grad_rows, preferred_element_type=jnp.float32
    )
    grad_scores = weights * (grad_weights - jnp.sum(weights * grad_weights, -1, keepdims=True))
    grad_raw = (grad_scores * queries.shape[-1] ** (-0.5)).astype(jnp.bfloat16)
    grad_queries = jnp.einsum(
        "hbk,khd->bhd", grad_raw, all_keys, preferred_element_type=jnp.float32
    )
    grad_keys = jnp.einsum("hbk,bhd->khd", grad_raw, queries, preferred_element_type=jnp.float32)
    return (grad_queries, grad_keys, grad_values)


def per_device(
    inputs,
    cotangent,
    norm_gain,
    qkv_weight,
    conv_kernel,
    persistent,
    out_weight,
    ffn_gain,
    gate_up,
    down_weight,
    memory_decay,
    momentum_decay,
    doc_start,
):
    full_rows, grad_rows_in, gain_one, gain_two = (
        lax.all_gather(inputs, "head", axis=1, tiled=True),
        lax.all_gather(cotangent, "head", axis=1, tiled=True),
        lax.all_gather(norm_gain, "head", axis=0, tiled=True),
        lax.all_gather(ffn_gain, "head", axis=0, tiled=True),
    )
    row_count, col_count = inputs.shape
    seq_rank = lax.axis_index("seq")
    head_rank = lax.axis_index("head")
    offset = seq_rank * row_count
    places = offset + jnp.arange(row_count, dtype=jnp.int32)
    local_width = qkv_weight.shape[2]
    head_count = local_width // DH
    fixed_count = persistent.shape[1]
    stream = full_rows.astype(jnp.float32)
    scale_one = lax.rsqrt(jnp.mean(stream * stream, -1, keepdims=True) + EPSILON)
    normed_one = stream * scale_one
    gain_first = gain_one.astype(jnp.float32)
    hidden_one = (normed_one * gain_first).astype(jnp.bfloat16)
    projected = jnp.einsum(
        "td,kdn->tkn", hidden_one, qkv_weight, preferred_element_type=jnp.float32
    ).reshape(row_count, 3 * local_width)
    edge_rows = KW - 1
    halo_rows = from_behind(projected[row_count - edge_rows :], "seq", 1)
    extended = jnp.concatenate([halo_rows, projected], 0)
    kernel = conv_kernel.reshape(KW, 3 * local_width)
    inside = [
        (places - shift_tap >= doc_start).astype(jnp.float32)[:, None] for shift_tap in range(KW)
    ]
    mixed_rows = jnp.zeros_like(projected)
    for shift_tap in range(KW):
        mixed_rows = (
            mixed_rows
            + kernel[shift_tap][None]
            * extended[edge_rows - shift_tap : edge_rows - shift_tap + row_count]
            * inside[shift_tap]
        )
    rounded = mixed_rows.astype(jnp.bfloat16).reshape(row_count, 3, head_count, DH)
    queries = rounded[:, 0]
    key_rows = rounded[:, 1]
    value_rows = rounded[:, 2]
    all_keys = jnp.concatenate([persistent[0].reshape(fixed_count, head_count, DH), key_rows], 0)
    all_values = jnp.concatenate(
        [persistent[1].reshape(fixed_count, head_count, DH), value_rows], 0
    )
    block_count = row_count // QBLK
    query_blocks = queries.reshape(block_count, QBLK, head_count, DH)
    row_blocks = jnp.arange(row_count, dtype=jnp.int32).reshape(block_count, QBLK)
    start_blocks = doc_start.reshape(block_count, QBLK)

    def forward_block(pieces):
        return attend_forward(
            pieces[0], pieces[1], pieces[2], all_keys, all_values, offset, fixed_count
        )

    attended, totals = lax.map(forward_block, (query_blocks, row_blocks, start_blocks))
    attended = attended.reshape(row_count, head_count, DH)
    query_float = queries.astype(jnp.float32)
    key_float = key_rows.astype(jnp.float32)
    value_float = value_rows.astype(jnp.float32)
    log_keep = jnp.log(memory_decay)
    log_carry = jnp.log(momentum_decay)

    def local_memory(query_in, key_in, value_in):
        return memory_local(query_in, key_in, value_in, log_keep, log_carry, doc_start, places)

    (
        (reading, mem_off, mom_off),
        local_pull,
        (keep_rows, cross_rows, keep_dev, cross_dev, carry_dev),
    ) = jax.vjp(local_memory, query_float, key_float, value_float, has_aux=True)
    zero_state = jnp.zeros((head_count, DH, DH), jnp.float32)
    identity = (
        jnp.ones((head_count,), jnp.float32),
        jnp.zeros((head_count,), jnp.float32),
        jnp.ones((head_count,), jnp.float32),
        zero_state,
        zero_state,
    )
    prefix = entering(
        (keep_dev, cross_dev, carry_dev, mem_off, mom_off), "seq", compose, identity, False
    )

    def incoming(query_in, memory_in, momentum_in):
        return correction(query_in, memory_in, momentum_in, keep_rows, cross_rows)

    added_read, incoming_pull = jax.vjp(incoming, query_float, prefix[3], prefix[4])
    memory_out = reading + added_read
    scale_mem = lax.rsqrt(jnp.mean(memory_out * memory_out, -1, keepdims=True) + MEMORY_FLOOR)
    normed_mem = memory_out * scale_mem
    merged = (attended + normed_mem).reshape(row_count, local_width).astype(jnp.bfloat16)
    mixer_part = jnp.dot(merged, out_weight, preferred_element_type=jnp.float32)
    gain_second = gain_two.astype(jnp.float32)
    branch = lax.psum(mixer_part.astype(jnp.bfloat16), "head").astype(jnp.float32)
    middle = stream + branch
    scale_two = lax.rsqrt(jnp.mean(middle * middle, -1, keepdims=True) + EPSILON)
    normed_two = middle * scale_two
    hidden_two = (normed_two * gain_second).astype(jnp.bfloat16)
    middle_share = lax.dynamic_slice_in_dim(middle, head_rank * col_count, col_count, 1)
    gated = jnp.einsum("td,kdf->tkf", hidden_two, gate_up, preferred_element_type=jnp.float32)
    gate_vals = gated[:, 0]
    up_vals = gated[:, 1]
    sigmoid_gate = jax.nn.sigmoid(gate_vals)
    silu_gate = gate_vals * sigmoid_gate
    activated = (silu_gate * up_vals).astype(jnp.bfloat16)
    ffn_share = lax.psum_scatter(
        jnp.dot(activated, down_weight, preferred_element_type=jnp.float32).astype(jnp.bfloat16),
        "head",
        scatter_dimension=1,
        tiled=True,
    ).astype(jnp.float32)
    output = (middle_share + ffn_share).astype(jnp.bfloat16)
    grad_act = jnp.einsum(
        "td,fd->tf", grad_rows_in, down_weight, preferred_element_type=jnp.float32
    )
    grad_down_full = jnp.einsum(
        "tf,td->fd", activated, grad_rows_in, preferred_element_type=jnp.float32
    )
    silu_slope = sigmoid_gate * (1.0 + gate_vals * (1.0 - sigmoid_gate))
    grad_gated = jnp.stack([grad_act * up_vals * silu_slope, grad_act * silu_gate], 1).astype(
        jnp.bfloat16
    )
    grad_gate_full = jnp.einsum(
        "td,tkf->kdf", hidden_two, grad_gated, preferred_element_type=jnp.float32
    )
    hidden_part = jnp.einsum("tkf,kdf->td", grad_gated, gate_up, preferred_element_type=jnp.float32)
    grad_hidden_two = lax.psum(hidden_part.astype(jnp.bfloat16), "head").astype(jnp.float32)
    grad_normed_two = grad_hidden_two * gain_second
    grad_gain_two = lax.dynamic_slice_in_dim(
        jnp.sum(grad_hidden_two * normed_two, 0), head_rank * col_count, col_count, 0
    )
    grad_middle = grad_rows_in.astype(jnp.float32) + scale_two * (
        grad_normed_two - normed_two * jnp.mean(grad_normed_two * normed_two, -1, keepdims=True)
    )
    grad_middle_low = grad_middle.astype(jnp.bfloat16)
    grad_middle_share = lax.dynamic_slice_in_dim(grad_middle, head_rank * col_count, col_count, 1)
    grad_merged = jnp.einsum(
        "td,nd->tn", grad_middle_low, out_weight, preferred_element_type=jnp.float32
    ).reshape(row_count, head_count, DH)
    grad_out_full = jnp.einsum(
        "tn,td->nd", merged, grad_middle_low, preferred_element_type=jnp.float32
    )
    grad_mem = scale_mem * (
        grad_merged - normed_mem * jnp.mean(grad_merged * normed_mem, -1, keepdims=True)
    )
    grad_query_in, grad_mem_in, grad_mom_in = incoming_pull(grad_mem)
    suffix = entering(
        (keep_dev, cross_dev, carry_dev, grad_mem_in, grad_mom_in), "seq", pull_back, identity, True
    )
    grad_query_mem, grad_key_mem, grad_value_mem = local_pull((grad_mem, suffix[3], suffix[4]))
    grad_att_low = grad_merged.astype(jnp.bfloat16).reshape(block_count, QBLK, head_count, DH)

    def backward_block(running, pieces):
        grad_query_part, grad_key_part, grad_value_part = attend_backward(
            pieces[0],
            pieces[1],
            pieces[2],
            all_keys,
            all_values,
            offset,
            fixed_count,
            pieces[3],
            pieces[4],
        )
        return ((running[0] + grad_key_part, running[1] + grad_value_part), grad_query_part)

    zero_keys = jnp.zeros((fixed_count + row_count, head_count, DH), jnp.float32)
    (grad_keys_all, grad_values_all), grad_query_blocks = lax.scan(
        backward_block,
        (zero_keys, zero_keys),
        (query_blocks, row_blocks, start_blocks, totals, grad_att_low),
    )
    grad_query_att = grad_query_blocks.reshape(row_count, head_count, DH)
    grad_mixed = jnp.stack(
        [
            grad_query_att + grad_query_mem + grad_query_in,
            grad_keys_all[fixed_count:] + grad_key_mem,
            grad_values_all[fixed_count:] + grad_value_mem,
        ],
        1,
    ).reshape(row_count, 3 * local_width)
    grad_extended = jnp.zeros_like(extended)
    kernel_rows = []
    for shift_tap in range(KW):
        tap_term = grad_mixed * inside[shift_tap]
        grad_extended = grad_extended + jnp.pad(
            kernel[shift_tap][None] * tap_term, ((edge_rows - shift_tap, shift_tap), (0, 0))
        )
        kernel_rows.append(
            jnp.sum(
                tap_term * extended[edge_rows - shift_tap : edge_rows - shift_tap + row_count], 0
            )
        )
    returned = from_behind(grad_extended[:edge_rows], "seq", -1)
    grad_projected = (
        (grad_extended[edge_rows:] + jnp.pad(returned, ((row_count - edge_rows, 0), (0, 0))))
        .astype(jnp.bfloat16)
        .reshape(row_count, 3, local_width)
    )
    grad_qkv_full = jnp.einsum(
        "td,tkn->kdn", hidden_one, grad_projected, preferred_element_type=jnp.float32
    )
    grad_hidden_one = jnp.einsum(
        "tkn,kdn->td", grad_projected, qkv_weight, preferred_element_type=jnp.float32
    )
    grad_normed_one = grad_hidden_one * gain_first
    grad_gain_part = jnp.sum(grad_hidden_one * normed_one, 0)
    grad_input_part = scale_one * (
        grad_normed_one - normed_one * jnp.mean(grad_normed_one * normed_one, -1, keepdims=True)
    )
    grad_input_share, grad_gain_one = (
        lax.psum_scatter(
            grad_input_part.astype(jnp.bfloat16), "head", scatter_dimension=1, tiled=True
        ).astype(jnp.float32),
        lax.psum_scatter(
            grad_gain_part.astype(jnp.bfloat16), "head", scatter_dimension=0, tiled=True
        ).astype(jnp.float32),
    )
    input_grad = grad_input_share + grad_middle_share
    grad_persistent = jnp.stack(
        [grad_keys_all[:fixed_count], grad_values_all[:fixed_count]], 0
    ).reshape(2, fixed_count, local_width)
    grad_kernel = jnp.stack(kernel_rows, 0).reshape(KW, 3, local_width)
    reduced_small = lax.psum((grad_gain_one, grad_gain_two, grad_kernel, grad_persistent), "seq")
    reduced_large = (
        lax.psum_scatter(grad_qkv_full, "seq", scatter_dimension=1, tiled=True),
        lax.psum_scatter(grad_out_full, "seq", scatter_dimension=1, tiled=True),
        lax.psum_scatter(grad_gate_full, "seq", scatter_dimension=1, tiled=True),
        lax.psum_scatter(grad_down_full, "seq", scatter_dimension=1, tiled=True),
    )
    return (
        output,
        input_grad,
        reduced_small[0],
        reduced_large[0],
        reduced_small[2],
        reduced_small[3],
        reduced_large[1],
        reduced_small[1],
        reduced_large[2],
        reduced_large[3],
    )


def solution(mesh):
    placed = (
        P("seq", "head"),
        P("seq", "head"),
        P("head"),
        P(None, None, "head"),
        P(None, None, "head"),
        P(None, None, "head"),
        P("head", None),
        P("head"),
        P(None, None, "head"),
        P("head", None),
        P("seq", "head"),
        P("seq", "head"),
        P("seq"),
    )
    return jax.shard_map(
        per_device,
        mesh=mesh,
        in_specs=placed,
        out_specs=(
            P("seq", "head"),
            P("seq", "head"),
            P("head"),
            P(None, "seq", "head"),
            P(None, None, "head"),
            P(None, None, "head"),
            P("head", "seq"),
            P("head"),
            P(None, "seq", "head"),
            P("head", "seq"),
        ),
        check_vma=False,
    )
```

profile of v0, /device:TPU:0, one launch (start us, length us, event | category | flops | bytes accessed | tf_op | source)
XLA Modules:
  0.0 1143.1 jit_solution(17869236885246516802)
XLA Ops:
  8.7 6.0 all-gather.7
  19.4 15.8 %all-gather.12.cloned.1.call-done = bf16[1024,1024]{1,0:T(8,128)(2,1)} async-done(((bf16[1024,256]{1,0:T(8,128)(2,1)}), bf16[1024,1024]{1,0:T(8,128)(2,1)}) %all-gather.12.cloned.1.call-update) | async-done | bytes 2097168 | tf_op jit(solution)/shard_map/all_gather | solution.py:225
  37.8 3.9 fusion.185
  44.3 3.6 collective-permute-start
  59.0 3.5 copy.127
  62.6 9.0 add_convert_fusion
  90.4 102.8 %while.126 = (s32[]{:T(128)}, f32[2,128,128]{2,1,0:T(8,128)S(1)}, f32[2,128,128]{2,1,0:T(8,128)S(1)}, f32[2]{0:T(128)}, f32[2]{0:T(128)S(1)}, /*index=5*/f32[2]{...) while((s32[]{:T(128)}, f32[2,128,128]{2,1,0:T(8,128)S(1)}, ...), condition=%wide.region_10.11_spmd.clone, body=%wide.region_5.10_spmd.clone.sunk | while | flops 607096064 | bytes 8804623 | solution.py:148
  197.0 19.3 %all-reduce.10 = (bf16[16]{0:T(256)(128)(2,1)S(1)}, bf16[16]{0:T(256)(128)(2,1)S(1)}, bf16[16]{0:T(256)(128)(2,1)S(1)}) all-reduce(bf16[16]{0:T(256)(128)(2,1)S(1)} %dynamic-update-slice, bf16[16]{0:T(256)(128)(2,1)S(1)} %dynamic-update-slice.1, bf16[16]{0:T(256)(128)(2,1)S(1)} %dynamic-update-slice.2), channel_id=2, replica_groups=mesh['seq'=8,'head'=4] {'seq'}, use_global_device_ids=true, to_apply=%add.5 | all-reduce | flops 48 | bytes 192
  217.8 33.4 %all-gather.4 = bf16[16,128,128]{2,1,0:T(8,128)(2,1)} all-gather(bf16[2,128,128]{2,1,0:T(8,128)(2,1)S(1)} %convert_element_type.293), channel_id=6, replica_groups=mesh['seq'=8,'head'=4] {'seq'}, dimensions={0}, use_global_device_ids=true | all-gather | bytes 589824 | tf_op jit(solution)/shard_map/all_gather | solution.py:30
  251.2 33.3 %all-gather.2 = bf16[16,128,128]{2,1,0:T(8,128)(2,1)} all-gather(bf16[2,128,128]{2,1,0:T(8,128)(2,1)S(1)} %convert_element_type.291), channel_id=4, replica_groups=mesh['seq'=8,'head'=4] {'seq'}, dimensions={0}, use_global_device_ids=true | all-gather | bytes 589824 | tf_op jit(solution)/shard_map/all_gather | solution.py:30
  300.0 36.4 %while.122 = (s32[]{:T(128)}, f32[2,512,2,128]{1,0,3,2:T(2,128)}, f32[2,2,512,1]{2,1,3,0:T(2,128)S(1)}, s32[2,512]{1,0:T(2,128)S(1)}, s32[]{:T(128)}, /*index=5*...) while((s32[]{:T(128)}, f32[2,512,2,128]{1,0,3,2:T(2,128)}, ...), condition=%wide.region_4.5_spmd, body=%wide.region_1.4_spmd.sunk | while | flops 555936576 | bytes 17871400 | solution.py:279
  307.8 10.4 dynamic_update_slice.109
  326.0 10.4 dynamic_update_slice.109
  346.2 5.5 all-gather.8
  351.6 48.6 %all-reduce.14.cloned.1.call-done = bf16[1024,1024]{1,0:T(8,128)(2,1)} async-done(((bf16[1024,1024]{1,0:T(8,128)(2,1)}), bf16[1024,1024]{1,0:T(8,128)(2,1)}) %all-reduce.14.cloned.1.call-update) | async-done | bytes 2097168 | tf_op jit(solution)/shard_map/psum | solution.py:317
  403.7 5.6 fusion.209
  409.3 15.5 %all-gather.14.cloned.1.call-done = bf16[1024,1024]{1,0:T(8,128)(2,1)} async-done(((bf16[1024,256]{1,0:T(8,128)(2,1)}), bf16[1024,1024]{1,0:T(8,128)(2,1)}) %all-gather.14.cloned.1.call-update) | async-done | bytes 2097168 | tf_op jit(solution)/shard_map/all_gather | solution.py:226
  424.9 7.5 fusion.177
  433.9 4.6 bitcast_convert_fusion
  438.6 5.1 convolution_convert_fusion.1
  443.8 46.3 %all-reduce.16.cloned.1.call-done = bf16[1024,1024]{1,0:T(8,128)(2,1)} async-done(((bf16[1024,1024]{1,0:T(8,128)(2,1)}), bf16[1024,1024]{1,0:T(8,128)(2,1)}) %all-reduce.16.cloned.1.call-update) | async-done | bytes 2097168 | tf_op jit(solution)/shard_map/psum | solution.py:350
  490.1 4.1 fusion.156
  508.3 72.0 %while.127 = (s32[]{:T(128)}, f32[1040,2,128]{2,0,1:T(8,128)}, f32[1040,2,128]{2,0,1:T(8,128)S(1)}, f32[2,512,2,128]{1,0,3,2:T(2,128)}, bf16[2,512,2,128]{3,1,2,...) while((s32[]{:T(128)}, f32[1040,2,128]{2,0,1:T(8,128)}, ...), condition=%wide.region_21.22_spmd.clone, body=%wide.region_19.21_spmd.clone.sunk | while | flops 1382350592 | bytes 70255272 | solution.py:391
  513.9 3.8 fusion.424
  517.7 7.7 fusion.427
  525.4 8.1 fusion.425
  533.9 10.4 dynamic_update_slice.117
  549.8 3.8 fusion.424
  553.6 7.6 fusion.427
  561.2 8.4 fusion.425
  570.0 10.4 dynamic_update_slice.117
  580.3 3.5 reshape.1149
  588.0 32.0 %all-gather.5 = bf16[16,128,128]{2,1,0:T(8,128)(2,1)S(1)} all-gather(bf16[2,128,128]{2,1,0:T(8,128)(2,1)S(1)} %convolution_convert_fusion.3), channel_id=7, replica_groups=mesh['seq'=8,'head'=4] {'seq'}, dimensions={0}, use_global_device_ids=true | all-gather | bytes 589824 | tf_op jit(solution)/shard_map/all_gather | solution.py:30
  620.0 31.2 %all-gather.6 = bf16[16,128,128]{2,1,0:T(8,128)(2,1)S(1)} all-gather(bf16[2,128,128]{2,1,0:T(8,128)(2,1)S(1)} %convolution_convert_fusion.2), channel_id=8, replica_groups=mesh['seq'=8,'head'=4] {'seq'}, dimensions={0}, use_global_device_ids=true | all-gather | bytes 589824 | tf_op jit(solution)/shard_map/all_gather | solution.py:30
  657.1 69.6 %while.125 = (s32[]{:T(128)}, f32[2,128,128]{2,1,0:T(8,128)S(1)}, f32[2,128,128]{2,1,0:T(8,128)S(1)}, f32[4,2,256,128]{3,2,1,0:T(8,128)}, f32[4,2,256,128]{3,2,1...) while((s32[]{:T(128)}, f32[2,128,128]{2,1,0:T(8,128)S(1)}, ...), condition=%wide.region_30.31_spmd, body=%wide.region_25.30_spmd.sunk | while | flops 1110835968 | bytes 17551356 | solution.py:148
  747.4 5.6 multiply_reduce_fusion.6
  757.4 5.5 collective-permute-done.1
  769.3 5.0 convolution_bitcast_fusion.3
  775.4 4.2 fusion.192
  779.9 5.3 fusion.224
  785.2 8.3 convolution_bitcast_fusion.2
  802.2 3.3 fusion.168
  805.6 5.7 all-reduce.8
  811.3 37.6 %all-reduce.9 = (f32[256]{0:T(256)}, f32[4,3,256]{2,1,0:T(4,128)S(1)}, f32[2,16,256]{2,1,0:T(8,128)}, f32[256]{0:T(256)}) all-reduce(f32[256]{0:T(256)S(1)} %dynamic-slice_convert_fusion, f32[4,3,256]{2,1,0:T(4,128)S(1)} %pad_maximum_fusion.8, f32[2,16,256]{2,1,0:T(8,128)S(1)} %pad_maximum_fusion.7, ...), channel_id=1, replica_groups=mesh['seq'=8,'head'=4] {'seq'}, use_global_device_ids=true, to_apply=%region_35.36 | all-reduce | flops 11776 | bytes 94208 | tf_op jit(solution)/shard_map/psum | solution.py:447
  854.3 24.7 %reduce-scatter.11.cloned.1.call-done = f32[3,128,256]{1,2,0:T(8,128)} async-done(((f32[3,1024,256]{1,2,0:T(8,128)}), f32[3,128,256]{1,2,0:T(8,128)}) %reduce-scatter.11.cloned.1.call-update) | async-done | bytes 393232 | tf_op jit(solution)/shard_map/reduce_scatter | solution.py:449
  880.9 65.3 %reduce-scatter.13.cloned.1.call-done = f32[256,128]{1,0:T(8,128)} async-done(((f32[256,1024]{1,0:T(8,128)}), f32[256,128]{1,0:T(8,128)}) %reduce-scatter.13.cloned.1.call-update) | async-done | bytes 131088 | tf_op jit(solution)/shard_map/reduce_scatter | solution.py:450
  946.2 75.8 %reduce-scatter.17.cloned.1.call-done = f32[704,128]{1,0:T(8,128)} async-done(((f32[704,1024]{1,0:T(8,128)}), f32[704,128]{1,0:T(8,128)}) %reduce-scatter.17.cloned.1.call-update) | async-done | bytes 360464 | tf_op jit(solution)/shard_map/reduce_scatter | solution.py:452
  1021.9 114.1 %reduce-scatter.15.cloned.1.call-done = f32[2,128,704]{1,2,0:T(8,128)} async-done(((f32[2,1024,704]{1,2,0:T(8,128)}), f32[2,128,704]{1,2,0:T(8,128)}) %reduce-scatter.15.cloned.1.call-update) | async-done | bytes 720912 | tf_op jit(solution)/shard_map/reduce_scatter | solution.py:451
  (841 shorter events, 347.0 us)
Async XLA Ops:
  7.2 396.2 %copy-start = (bf16[2,1024,704]{1,2,0:T(8,128)(2,1)S(1)}, bf16[2,1024,704]{1,2,0:T(8,128)(2,1)}, u32[]{:S(2)}) copy-start(bf16[2,1024,704]{1,2,0:T(8,128)(2,1)} %param.33) | copy-start | bytes 8650756
  7.2 28.0 %all-gather.12.cloned.1.call-start = ((), (), s32[]{:S(2)}) async-start(), calls=%async_computation.6 | async-start | bytes 2621440 | tf_op jit(solution)/shard_map/all_gather | solution.py:225
  7.9 392.3 %all-reduce.14.cloned.1.call-start = ((), (), s32[]{:S(2)}) async-start(), calls=%async_computation.7 | async-start | bytes 4194304 | tf_op jit(solution)/shard_map/psum | solution.py:317
  14.7 22.6 %copy-start.73 = (f32[4,1,256]{2,1,0:T(1,128)}, f32[4,1,256]{2,1,0:T(1,128)S(1)}, u32[]{:S(2)}) copy-start(f32[4,1,256]{2,1,0:T(1,128)S(1)} %convert_element_type.327) | copy-start | bytes 12292
  18.1 44.5 %copy-start.59 = (f32[1024]{0:T(1024)}, f32[1024]{0:T(1024)S(1)}, u32[]{:S(2)}) copy-start(f32[1024]{0:T(1024)S(1)} %get-tuple-element.1656) | copy-start | bytes 12292
  37.8 10.7 copy-start.72
  44.3 18.3 %collective-permute-start = (f32[3,768]{0,1:T(8,128)}, f32[3,768]{0,1:T(8,128)S(1)}, u32[]{:S(2)}, u32[]{:S(2)}) collective-permute-start(f32[3,768]{0,1:T(8,128)} %copy.128), channel_id=1, source_target_pairs={{0,4},{4,8},{8,12},{12,16},{16,20},{20,24},{24,28},{1,5},{5,9},{9,... | collective-permute-start | bytes 27656 | tf_op jit(solution)/shard_map/ppermute | solution.py:22
  52.3 10.3 copy-start.62
  52.3 10.3 copy-start.64
  53.0 9.6 copy-start.66
  62.6 12.1 %copy-start.47 = (f32[3,768]{0,1:T(8,128)}, f32[3,768]{0,1:T(8,128)S(1)}, u32[]{:S(2)}) copy-start(f32[3,768]{0,1:T(8,128)S(1)} %collective-permute-done) | copy-start | bytes 27652
  82.0 8.4 copy-start.77
  108.1 7.1 copy-start.79
  118.3 5.3 copy-start.53
  134.0 7.1 copy-start.79
  144.3 5.3 copy-start.53
  160.1 7.1 copy-start.79
  170.3 5.3 copy-start.53
  186.1 7.1 copy-start.79
  284.5 5.7 copy-start.58
  284.8 10.1 copy-start.26
  284.8 10.0 copy-start.28
  294.8 5.2 copy-start.55
  345.4 79.5 %all-gather.14.cloned.1.call-start = ((), (), s32[]{:S(2)}) async-start(), calls=%async_computation.9 | async-start | bytes 2621440 | tf_op jit(solution)/shard_map/all_gather | solution.py:226
  346.1 144.0 %all-reduce.16.cloned.1.call-start = ((), (), s32[]{:S(2)}) async-start(), calls=%async_computation.10 | async-start | bytes 4194304 | tf_op jit(solution)/shard_map/psum | solution.py:350
  438.6 411.0 %reduce-scatter.7.cloned.1.call-start = ((), (), s32[]{:S(2)}) async-start(), calls=%async_computation.8 | async-start | bytes 2621440 | tf_op jit(solution)/shard_map/reduce_scatter | solution.py:329
  443.7 46.4 %copy-start.4 = (bf16[1024,1024]{1,0:T(8,128)(2,1)S(1)}, bf16[1024,1024]{1,0:T(8,128)(2,1)}, u32[]{:S(2)}) copy-start(bf16[1024,1024]{1,0:T(8,128)(2,1)} %all-gather.12.cloned.1.call-done) | copy-start | bytes 6291460
  443.8 408.1 %reduce-scatter.9.cloned.1.call-start = ((), (), s32[]{:S(2)}) async-start(), calls=%async_computation.11 | async-start | bytes 2621440 | tf_op jit(solution)/shard_map/reduce_scatter | solution.py:435
  501.9 6.4 copy-start.7
  517.7 7.7 copy-start.50
  553.6 7.7 copy-start.50
  580.3 7.6 copy-start.8
  585.3 67.2 %copy-start.36 = (f32[4,256,2,128]{1,0,3,2:T(4,128)S(1)}, f32[4,256,2,128]{1,0,3,2:T(4,128)}, u32[]{:S(2)}) copy-start(f32[4,256,2,128]{1,0,3,2:T(4,128)} %reshape.1151) | copy-start | bytes 3145732
  726.7 5.5 copy-start.38
  729.3 7.1 copy-start.37
  733.5 7.0 copy-start.10
  733.5 7.0 copy-start.27
  753.2 9.7 collective-permute-start.1
  757.3 6.4 copy-start.5
  757.4 6.4 copy-start.74
  757.4 6.4 copy-start.76
  757.4 6.4 copy-start.81
  769.2 109.8 %reduce-scatter.11.cloned.1.call-start = ((), (), s32[]{:S(2)}) async-start(), calls=%async_computation.12 | async-start | bytes 3538944 | tf_op jit(solution)/shard_map/reduce_scatter | solution.py:449
  774.3 171.9 %reduce-scatter.13.cloned.1.call-start = ((), (), s32[]{:S(2)}) async-start(), calls=%async_computation.13 | async-start | bytes 1179648 | tf_op jit(solution)/shard_map/reduce_scatter | solution.py:450
  779.6 242.3 %reduce-scatter.17.cloned.1.call-start = ((), (), s32[]{:S(2)}) async-start(), calls=%async_computation.15 | async-start | bytes 3244032 | tf_op jit(solution)/shard_map/reduce_scatter | solution.py:452
  785.2 350.8 %reduce-scatter.15.cloned.1.call-start = ((), (), s32[]{:S(2)}) async-start(), calls=%async_computation.14 | async-start | bytes 6488064 | tf_op jit(solution)/shard_map/reduce_scatter | solution.py:451
  793.5 7.3 copy-start.21
  802.2 333.8 %copy-start.1 = (bf16[2,1024,704]{1,2,0:T(8,128)(2,1)S(1)}, bf16[2,1024,704]{1,2,0:T(8,128)(2,1)}, u32[]{:S(2)}) copy-start(bf16[2,1024,704]{1,2,0:T(8,128)(2,1)} %param.33) | copy-start | bytes 8650756
  (83 other events, 254.7 us)
Sparse Core Ops, SparseCore 0:
  9.6 25.5 all-gather.11
  345.5 54.7 all-reduce.13
  401.9 22.9 all-gather.13
  438.7 51.3 all-reduce.15
  492.5 31.5 reduce-scatter.6
  769.3 29.6 reduce-scatter.8
  802.7 76.2 reduce-scatter.10
  883.0 63.1 reduce-scatter.12
  950.8 71.1 reduce-scatter.16
  1026.5 109.4 reduce-scatter.14
where the time goes:
time: 1150 us; the launch traced here: 1140 us
  waiting for transfers between devices  413 us (36%)
  blocking collectives  204 us (18%)
  local copies, waits for them, and re-layouts  197 us (17%)
  matrix products  194 us (17%)
  other arithmetic  110 us (10%)
  between operations  16.7 us (1%)
    all_gather x4, blocking collectives, entering(): lax.all_gather(a.astype(kind), axis)  130 us
    reduce_scatter x1, waiting for transfers between devices, per_device(): lax.psum_scatter(grad_gate_full, 'seq', scatter_dimension=1, tiled=True)  114 us
    reduce_scatter x1, waiting for transfers between devices, per_device(): lax.psum_scatter(grad_down_full, 'seq', scatter_dimension=1, tiled=True)  75.8 us
    reduce_scatter x1, waiting for transfers between devices, per_device(): lax.psum_scatter(grad_out_full, 'seq', scatter_dimension=1, tiled=True)  65.3 us
    psum x1, waiting for transfers between devices, per_device(): lax.psum(mixer_part.astype(jnp.bfloat16), 'head').astype(jnp.float32)  48.6 us
    psum x1, waiting for transfers between devices, per_device(): lax.psum(hidden_part.astype(jnp.bfloat16), 'head').astype(jnp.float32)  46.3 us
    dynamic_update_slice x8, local copies, waits for them, and re-layouts, per_device(): lax.map(forward_block, (query_blocks, row_blocks, start_blocks))  46.2 us
    psum x1, blocking collectives, per_device(): lax.psum((grad_gain_one, grad_gain_two, grad_kernel, grad_persistent), 's...  37.6 us
  transfers between devices with their start and end apart: 12, of which 9 were waited for; matrix products, arithmetic and copies ran while one was open for 24% of the time, Pallas kernels for 0%

commit v1 on v0

v1 whole, which is shorter than its diff:
```python
import functools

import jax
import jax.numpy as jnp
from jax import lax
from jax.experimental import pallas as pl
from jax.experimental.pallas import tpu as pltpu
from jax.sharding import PartitionSpec as P

DH = 128
KW = 4
SEG = 1024
MBLK = 256
EPSILON = 1e-06
MEMORY_FLOOR = 64.0
MASKED = -1e30
F32 = jnp.float32
BF16 = jnp.bfloat16
NN = (((1,), (0,)), ((), ()))
NT = (((1,), (1,)), ((), ()))
TN = (((0,), (0,)), ((), ()))
REL = 4


def mm(a, b, dims=NN):
    return lax.dot_general(a, b, dims, preferred_element_type=F32)


def exact(a, b, dims=NN):
    return lax.dot_general(
        a, b, dims, precision=lax.Precision.HIGHEST, preferred_element_type=F32
    )


def call(kernel, grid, in_specs, out_specs, out_shape, scratch=(), flops=0, moved=0, prefetch=0):
    spec = pltpu.PrefetchScalarGridSpec(
        num_scalar_prefetch=prefetch,
        grid=grid,
        in_specs=in_specs,
        out_specs=out_specs,
        scratch_shapes=list(scratch),
    )
    return pl.pallas_call(
        kernel,
        grid_spec=spec,
        out_shape=out_shape,
        compiler_params=pltpu.CompilerParams(vmem_limit_bytes=56 * 2**20),
        cost_estimate=pl.CostEstimate(
            flops=int(flops), bytes_accessed=int(moved), transcendentals=0
        ),
    )


def whole(shape):
    return pl.BlockSpec(shape, lambda *_: (0,) * len(shape))


def sds(shape, dtype):
    return jax.ShapeDtypeStruct(shape, dtype)


def iota(shape, dim):
    return lax.broadcasted_iota(jnp.int32, shape, dim)


def swap(x, axis, bit):
    count = lax.axis_size(axis)
    return lax.ppermute(x, axis, [(i, i ^ bit) for i in range(count)])


def shifted(x, axis, by):
    count = lax.axis_size(axis)
    return lax.ppermute(x, axis, [(i, i + by) for i in range(count) if 0 <= i + by < count])


def gather_rel(x):
    far = swap(x, "head", 2)
    near = swap(x, "head", 1)
    return [x, near, far, swap(far, "head", 1)]


def sum_over(x, axis):
    bit = 1
    while bit < lax.axis_size(axis):
        x = x + swap(x, axis, bit)
        bit *= 2
    return x


def front_kernel(rank_ref, *refs, heads):
    blocks, smalls = refs[:REL], refs[REL : 2 * REL]
    (
        w_ref,
        conv_ref,
        starts_ref,
        decay_ref,
        x_out,
        hid_out,
        scale_out,
        proj_out,
        qkv_out,
        kmat_out,
        aux_out,
        part_out,
        halo_out,
        gain_out,
        state_out,
        load_out,
        small_sc,
        proj_sc,
        state_sc,
    ) = refs[2 * REL :]
    b = pl.program_id(0)
    rank = rank_ref[0]
    rows, width = blocks[0].shape
    local = heads * DH
    spans = [pl.ds(pl.multiple_of((rank ^ k) * width, width), width) for k in range(REL)]
    for k in range(REL):
        x_out[:, spans[k]] = blocks[k][...]
    scal = 2 * heads * DH

    @pl.when(b == 0)
    def _():
        for k in range(REL):
            small_sc[:, spans[k]] = smalls[k][...]
        small = small_sc[...].astype(F32)
        gain_out[...] = small
        scale = lax.rsqrt(jnp.mean(small * small, -1, keepdims=True) + EPSILON)
        hidden = (small * scale * small[8:9]).astype(BF16)
        for c in range(3):
            proj_sc[0:8, c * local : (c + 1) * local] = mm(hidden, w_ref[c])[0:8]
        halo_out[...] = proj_sc[0:8]
        state_sc[0:scal] = jnp.zeros((scal, DH), F32)
        row = iota((8, DH), 0)
        state_sc[scal : scal + 8] = jnp.where(
            (row < heads) | ((row >= 2 * heads) & (row < 3 * heads)), 1.0, 0.0
        ).astype(F32)

    gain = gain_out[8:9]
    x = x_out[...].astype(F32)
    scale = lax.rsqrt(jnp.mean(x * x, -1, keepdims=True) + EPSILON)
    hidden = (x * scale * gain).astype(BF16)
    hid_out[...] = hidden
    scale_out[...] = scale
    for c in range(3):
        proj_sc[8 : 8 + rows, c * local : (c + 1) * local] = mm(hidden, w_ref[c])
    base = b * rows
    place = base + iota((rows, 1), 0)
    starts = starts_ref[...]
    mixed = jnp.zeros((rows, 3 * local), F32)
    for j in range(KW):
        inside = (place - j >= starts).astype(F32)
        mixed = mixed + conv_ref[j : j + 1] * proj_sc[8 - j : 8 - j + rows] * inside
    rounded = mixed.astype(BF16)
    qkv_out[...] = rounded
    proj_out[...] = proj_sc[8 : 8 + rows].astype(BF16)
    proj_sc[0:8] = proj_sc[rows : rows + 8]

    logs = jnp.log(decay_ref[...])
    below = iota((rows, rows), 0)
    right = iota((rows, rows), 1)
    rows_sum = exact(logs, (below <= right).astype(F32))
    cols_sum = exact((right <= below).astype(F32), logs, NT)
    linked = (right <= below) & (base + right >= starts)
    fresh = starts < base
    last_start = starts[rows - 1 : rows]
    reaches_end = place >= last_start
    last_row = (iota((rows, DH), 0) == rows - 1).astype(BF16)
    lane = iota((rows, DH), 1)
    aux = jnp.zeros((rows, DH), F32)
    for h in range(heads):
        keep_col, keep_row = cols_sum[:, h : h + 1], rows_sum[h : h + 1]
        carry_col = cols_sum[:, heads + h : heads + h + 1]
        carry_row = rows_sum[heads + h : heads + h + 1]
        keep_mat = jnp.where(linked, jnp.exp(jnp.minimum(keep_col - keep_row, 0.0)), 0.0)
        carry_mat = jnp.where(linked, jnp.exp(jnp.minimum(carry_col - carry_row, 0.0)), 0.0)
        keep_low = keep_mat.astype(BF16)
        kernel = mm(keep_low, carry_mat.astype(BF16)).astype(BF16)
        kmat_out[h, 0] = kernel
        keep_weight = jnp.where(fresh, jnp.exp(keep_col), 0.0)
        carried = jnp.where(fresh, jnp.exp(carry_col), 0.0)
        cross = mm(keep_low, jnp.broadcast_to(carried, (rows, DH)).astype(BF16))
        end_kernel = mm(kernel, last_row, TN)
        end_carry = jnp.where(
            reaches_end, jnp.exp(jnp.minimum(carry_col[rows - 1 : rows] - carry_col, 0.0)), 0.0
        )
        for slot, column in enumerate((keep_weight, cross, carried, end_kernel, end_carry)):
            aux = jnp.where(lane == slot * heads + h, column, aux)
        keys = rounded[:, local + h * DH : local + (h + 1) * DH]
        values = rounded[:, 2 * local + h * DH : 2 * local + (h + 1) * DH].astype(F32)
        mem_part = mm((values * end_kernel).astype(BF16), keys, TN)
        mom_part = mm((values * end_carry).astype(BF16), keys, TN)
        lo, mid = h * DH, (heads + h) * DH
        part_out[0, lo : lo + DH] = mem_part
        part_out[0, mid : mid + DH] = mom_part
        keep_end = jnp.broadcast_to(keep_weight[rows - 1 : rows], (1, DH))
        cross_end = cross[rows - 1 : rows]
        carry_end = jnp.broadcast_to(carried[rows - 1 : rows], (1, DH))
        memory, momentum = state_sc[lo : lo + DH], state_sc[mid : mid + DH]
        state_sc[lo : lo + DH] = keep_end * memory + cross_end * momentum + mem_part
        state_sc[mid : mid + DH] = carry_end * momentum + mom_part
        keep_at, cross_at, carry_at = scal + h, scal + heads + h, scal + 2 * heads + h
        keep_dev = state_sc[keep_at : keep_at + 1]
        cross_dev = state_sc[cross_at : cross_at + 1]
        carry_dev = state_sc[carry_at : carry_at + 1]
        state_sc[keep_at : keep_at + 1] = keep_end * keep_dev
        state_sc[cross_at : cross_at + 1] = keep_end * cross_dev + cross_end * carry_dev
        state_sc[carry_at : carry_at + 1] = carry_end * carry_dev
    aux_out[...] = aux

    @pl.when(b == pl.num_programs(0) - 1)
    def _():
        state_out[...] = state_sc[...]
        pack_load(load_out, state_sc[...], scal)


def pack_load(load_out, state, scal):
    load_out[0:scal] = state[0:scal].astype(BF16)
    tail = state[scal : scal + 8]
    high = tail.astype(BF16).astype(F32)
    load_out[scal : scal + 16] = jnp.concatenate([high, tail - high], 0).astype(BF16)


def unpack(ref, scal):
    if ref.dtype == F32:
        return ref[0:scal], ref[scal : scal + 8]
    tail = ref[scal : scal + 16].astype(F32)
    return ref[0:scal].astype(F32), tail[0:8] + tail[8:16]


def front(rank, blocks, smalls, weight, conv, starts, decays, heads):
    total, width = blocks[0].shape
    model = width * REL
    local = heads * DH
    count = total // MBLK
    scal = 2 * heads * DH
    at = lambda b, *_: (b, 0)
    return call(
        functools.partial(front_kernel, heads=heads),
        (count,),
        [pl.BlockSpec((MBLK, width), at)] * REL
        + [whole(smalls[0].shape)] * REL
        + [
            whole(weight.shape),
            whole(conv.shape),
            pl.BlockSpec((MBLK, 1), at),
            pl.BlockSpec((8, MBLK), lambda b, *_: (0, b)),
        ],
        [
            pl.BlockSpec((MBLK, model), at),
            pl.BlockSpec((MBLK, model), at),
            pl.BlockSpec((MBLK, 1), at),
            pl.BlockSpec((MBLK, 3 * local), at),
            pl.BlockSpec((MBLK, 3 * local), at),
            pl.BlockSpec((heads, 1, MBLK, MBLK), lambda b, *_: (0, b, 0, 0)),
            pl.BlockSpec((MBLK, DH), at),
            pl.BlockSpec((1, scal, DH), lambda b, *_: (b, 0, 0)),
            whole((8, 3 * local)),
            whole((16, model)),
            whole((scal + 8, DH)),
            whole((scal + 16, DH)),
        ],
        [
            sds((total, model), BF16),
            sds((total, model), BF16),
            sds((total, 1), F32),
            sds((total, 3 * local), BF16),
            sds((total, 3 * local), BF16),
            sds((heads, count, MBLK, MBLK), BF16),
            sds((total, DH), F32),
            sds((count, scal, DH), F32),
            sds((8, 3 * local), F32),
            sds((16, model), F32),
            sds((scal + 8, DH), F32),
            sds((scal + 16, DH), BF16),
        ],
        [
            pltpu.VMEM((16, model), BF16),
            pltpu.VMEM((MBLK + 8, 3 * local), F32),
            pltpu.VMEM((scal + 8, DH), F32),
        ],
        flops=2.2e9,
        moved=12e6,
        prefetch=1,
    )(rank, *blocks, *smalls, weight, conv, starts, decays)


def join_kernel(first_ref, second_ref, state_out, load_out, *, heads, backward):
    scal = 2 * heads * DH
    first, first_tail = unpack(first_ref, scal)
    second, second_tail = unpack(second_ref, scal)
    tail = []
    for h in range(heads):
        lo, mid = h * DH, (heads + h) * DH
        keep_one, keep_two = first_tail[h : h + 1], second_tail[h : h + 1]
        cross_one, cross_two = (
            first_tail[heads + h : heads + h + 1],
            second_tail[heads + h : heads + h + 1],
        )
        carry_one, carry_two = (
            first_tail[2 * heads + h : 2 * heads + h + 1],
            second_tail[2 * heads + h : 2 * heads + h + 1],
        )
        mem_one, mom_one = first[lo : lo + DH], first[mid : mid + DH]
        mem_two, mom_two = second[lo : lo + DH], second[mid : mid + DH]
        if backward:
            state_out[lo : lo + DH] = mem_two + keep_two * mem_one
            state_out[mid : mid + DH] = mom_two + cross_two * mem_one + carry_two * mom_one
            cross = cross_two * keep_one + carry_two * cross_one
        else:
            state_out[lo : lo + DH] = keep_two * mem_one + cross_two * mom_one + mem_two
            state_out[mid : mid + DH] = carry_two * mom_one + mom_two
            cross = keep_two * cross_one + cross_two * carry_one
        state_out[scal + h : scal + h + 1] = keep_two * keep_one
        state_out[scal + heads + h : scal + heads + h + 1] = cross
        state_out[scal + 2 * heads + h : scal + 2 * heads + h + 1] = carry_two * carry_one
    for spare in range(3 * heads, 8):
        state_out[scal + spare : scal + spare + 1] = jnp.zeros((1, DH), F32)
    pack_load(load_out, state_out[...], scal)


def join(first, second, heads, backward):
    scal = 2 * heads * DH
    return call(
        functools.partial(join_kernel, heads=heads, backward=backward),
        (1,),
        [whole(first.shape), whole(second.shape)],
        [whole((scal + 8, DH)), whole((scal + 16, DH))],
        [sds((scal + 8, DH), F32), sds((scal + 16, DH), BF16)],
        flops=1e6,
        moved=1e6,
    )(first, second)


def entering(load, heads, backward):
    count = lax.axis_size("seq")
    sign = -1 if backward else 1
    one = shifted(load, "seq", sign)
    two = shifted(load, "seq", 2 * sign)
    covered = 2
    state, load = join(two, one, heads, backward)
    while covered < count - 1:
        state, load = join(shifted(load, "seq", covered * sign), state, heads, backward)
        covered *= 2
    return state


def attend_kernel(q_ref, k_ref, v_ref, fix_ref, starts_ref, kmat_ref, *outs):
    att_out, ratio_out, intra_out, prob_out, fixp_out = outs
    total = q_ref.shape[0]
    fixed_keys, fixed_values = fix_ref[0], fix_ref[1]
    factor = DH ** (-0.5)
    for i in range(total // MBLK):
        span = slice(i * MBLK, (i + 1) * MBLK)
        seen = (i + 1) * MBLK
        query = q_ref[span]
        raw = mm(query, k_ref[0:seen], NT)
        fixed = mm(query, fixed_keys, NT)
        key_at = iota((MBLK, seen), 1)
        ok = (key_at >= starts_ref[span]) & (key_at <= i * MBLK + iota((MBLK, seen), 0))
        raw = jnp.where(ok, raw, MASKED)
        top = jnp.maximum(jnp.max(raw, -1, keepdims=True), jnp.max(fixed, -1, keepdims=True))
        weights = jnp.exp((raw - top) * factor)
        fix_weights = jnp.exp((fixed - top) * factor)
        scale = 1.0 / (
            jnp.sum(weights, -1, keepdims=True) + jnp.sum(fix_weights, -1, keepdims=True)
        )
        low = (weights * scale).astype(BF16)
        fix_low = (fix_weights * scale).astype(BF16)
        prob_out[span, 0:seen] = low
        fixp_out[span] = fix_low
        attended = mm(low, v_ref[0:seen]) + mm(fix_low, fixed_values)
        held = jnp.sum(low.astype(F32), -1, keepdims=True) + jnp.sum(
            fix_low.astype(F32), -1, keepdims=True
        )
        att_out[span] = attended
        ratio_out[span] = attended / held
        near = mm(query, k_ref[span], NT)
        kernel = kmat_ref[0, i].astype(F32)
        intra_out[span] = mm((kernel * near).astype(BF16), v_ref[span])


def attend(qkv, fixed, starts, kmat, head, heads):
    total = qkv.shape[0]
    count = total // MBLK
    fixed_count = fixed.shape[1]
    lanes = lambda c: pl.BlockSpec((total, DH), lambda *_: (0, c * heads + head))
    return call(
        attend_kernel,
        (1,),
        [
            lanes(0),
            lanes(1),
            lanes(2),
            pl.BlockSpec((2, fixed_count, DH), lambda *_: (0, 0, head)),
            whole((total, 1)),
            pl.BlockSpec((1, count, MBLK, MBLK), lambda *_: (head, 0, 0, 0)),
        ],
        [whole((total, DH))] * 3 + [whole((total, total)), whole((total, fixed_count))],
        [sds((total, DH), F32)] * 3
        + [sds((total, total), BF16), sds((total, fixed_count), BF16)],
        flops=1.5e9,
        moved=8e6,
    )(qkv, qkv, qkv, fixed, starts, kmat)


def attend_back_kernel(
    q_ref, k_ref, v_ref, fix_ref, prob_ref, fixp_ref, ratio_ref, grad_ref, gmem_ref, kmat_ref, *outs
):
    dq_out, dk_out, dv_out, dfix_out, dqm_out, dkm_out, dvm_out = outs
    total = q_ref.shape[0]
    fixed_keys, fixed_values = fix_ref[0], fix_ref[1]
    factor = DH ** (-0.5)
    dfix_k = jnp.zeros(fixed_keys.shape, F32)
    dfix_v = jnp.zeros(fixed_keys.shape, F32)
    for i in reversed(range(total // MBLK)):
        span = slice(i * MBLK, (i + 1) * MBLK)
        seen = (i + 1) * MBLK
        query, grad = q_ref[span], grad_ref[span]
        delta = jnp.sum(grad.astype(F32) * ratio_ref[span], -1, keepdims=True)
        low, fix_low = prob_ref[span, 0:seen], fixp_ref[span]
        back = mm(grad, v_ref[0:seen], NT)
        fix_back = mm(grad, fixed_values, NT)
        grad_raw = (low.astype(F32) * (back - delta) * factor).astype(BF16)
        fix_raw = (fix_low.astype(F32) * (fix_back - delta) * factor).astype(BF16)
        dq_out[span] = mm(grad_raw, k_ref[0:seen]) + mm(fix_raw, fixed_keys)
        dk, dv = mm(grad_raw, query, TN), mm(low, grad, TN)
        if seen == total:
            dk_out[...] = dk
            dv_out[...] = dv
        else:
            dk_out[0:seen] += dk
            dv_out[0:seen] += dv
        dfix_k += mm(fix_raw, query, TN)
        dfix_v += mm(fix_low, grad, TN)
        keys, values, gmem = k_ref[span], v_ref[span], gmem_ref[span]
        kernel = kmat_ref[0, i].astype(F32)
        near = (kernel * mm(query, keys, NT)).astype(BF16)
        cross = (kernel * mm(gmem, values, NT)).astype(BF16)
        dqm_out[span] = mm(cross, keys)
        dkm_out[span] = mm(cross, query, TN)
        dvm_out[span] = mm(near, gmem, TN)
    dfix_out[0] = dfix_k
    dfix_out[1] = dfix_v


def attend_back(qkv, fixed, prob, fixp, ratio, grads, gmem, kmat, head, heads):
    total = qkv.shape[0]
    count = total // MBLK
    fixed_count = fixed.shape[1]
    lanes = lambda c: pl.BlockSpec((total, DH), lambda *_: (0, c * heads + head))
    return call(
        attend_back_kernel,
        (1,),
        [
            lanes(0),
            lanes(1),
            lanes(2),
            pl.BlockSpec((2, fixed_count, DH), lambda *_: (0, 0, head)),
            whole((total, total)),
            whole((total, fixed_count)),
            whole((total, DH)),
            lanes(0),
            lanes(0),
            pl.BlockSpec((1, count, MBLK, MBLK), lambda *_: (head, 0, 0, 0)),
        ],
        [whole((total, DH))] * 3 + [whole((2, fixed_count, DH))] + [whole((total, DH))] * 3,
        [sds((total, DH), F32)] * 3
        + [sds((2, fixed_count, DH), F32)]
        + [sds((total, DH), F32)] * 3,
        flops=3e9,
        moved=10e6,
    )(qkv, qkv, qkv, fixed, prob, fixp, ratio, grads, gmem, kmat)


def merge_kernel(q_ref, *refs, heads):
    atts, intras = refs[:heads], refs[heads : 2 * heads]
    aux_ref, part_ref, state_ref, merged_out, normed_out, scale_out, state_low, state_sc = refs[
        2 * heads :
    ]
    rows = q_ref.shape[0]
    lane = iota((rows, DH), 1)
    scales = jnp.zeros((rows, DH), F32)

    @pl.when(pl.program_id(0) == 0)
    def _():
        state_sc[...] = state_ref[0 : state_sc.shape[0]]

    for h in range(heads):
        lo, mid = h * DH, (heads + h) * DH
        memory, momentum = state_sc[lo : lo + DH], state_sc[mid : mid + DH]
        memory_low, momentum_low = memory.astype(BF16), momentum.astype(BF16)
        state_low[0, lo : lo + DH] = memory_low
        state_low[0, mid : mid + DH] = momentum_low
        query = q_ref[:, lo : lo + DH]
        keep = aux_ref[:, h : h + 1]
        cross = aux_ref[:, heads + h : heads + h + 1]
        carry = aux_ref[:, 2 * heads + h : 2 * heads + h + 1]
        out = (
            intras[h][...]
            + keep * mm(query, memory_low, NT)
            + cross * mm(query, momentum_low, NT)
        )
        scale = lax.rsqrt(jnp.mean(out * out, -1, keepdims=True) + MEMORY_FLOOR)
        normed = out * scale
        normed_out[:, lo : lo + DH] = normed
        scales = jnp.where(lane == h, scale, scales)
        merged_out[:, lo : lo + DH] = (atts[h][...] + normed).astype(BF16)
        end = slice(rows - 1, rows)
        state_sc[lo : lo + DH] = (
            keep[end] * memory + cross[end] * momentum + part_ref[0, lo : lo + DH]
        )
        state_sc[mid : mid + DH] = carry[end] * momentum + part_ref[0, mid : mid + DH]
    scale_out[...] = scales


def merge(qkv, atts, intras, aux, parts, state, heads):
    total = qkv.shape[0]
    count = total // MBLK
    local = heads * DH
    scal = 2 * local
    at = lambda b, *_: (b, 0)
    by_block = pl.BlockSpec((1, scal, DH), lambda b, *_: (b, 0, 0))
    return call(
        functools.partial(merge_kernel, heads=heads),
        (count,),
        [pl.BlockSpec((MBLK, local), at)]
        + [pl.BlockSpec((MBLK, DH), at)] * (2 * heads + 1)
        + [by_block, whole(state.shape)],
        [
            pl.BlockSpec((MBLK, local), at),
            pl.BlockSpec((MBLK, local), at),
            pl.BlockSpec((MBLK, DH), at),
            by_block,
        ],
        [
            sds((total, local), BF16),
            sds((total, local), F32),
            sds((total, DH), F32),
            sds((count, scal, DH), BF16),
        ],
        [pltpu.VMEM((scal, DH), F32)],
        flops=3e8,
        moved=6e6,
    )(qkv, *atts, *intras, aux, parts, state)


def middle_kernel(rank_ref, *refs):
    merged, weights = refs[:REL], refs[REL : 2 * REL]
    x_ref, gain_ref, hid_out, normed_out, scale_out, share_out, mid_sc = refs[2 * REL :]
    width = share_out.shape[1]
    middle = x_ref[...].astype(F32)
    for k in range(REL):
        middle = middle + mm(merged[k][...], weights[k][...])
    mid_sc[...] = middle
    scale = lax.rsqrt(jnp.mean(middle * middle, -1, keepdims=True) + EPSILON)
    normed = middle * scale
    normed_out[...] = normed.astype(BF16)
    hid_out[...] = (normed * gain_ref[9:10]).astype(BF16)
    scale_out[...] = scale
    share_out[...] = mid_sc[:, pl.ds(pl.multiple_of(rank_ref[0] * width, width), width)]


def middle(rank, merged, weights, x, gains):
    total, model = x.shape
    local = merged[0].shape[1]
    width = model // REL
    at = lambda b, *_: (b, 0)
    return call(
        middle_kernel,
        (total // MBLK,),
        [pl.BlockSpec((MBLK, local), at)] * REL
        + [whole(weights[0].shape)] * REL
        + [pl.BlockSpec((MBLK, model), at), whole(gains.shape)],
        [
            pl.BlockSpec((MBLK, model), at),
            pl.BlockSpec((MBLK, model), at),
            pl.BlockSpec((MBLK, 1), at),
            pl.BlockSpec((MBLK, width), at),
        ],
        [
            sds((total, model), BF16),
            sds((total, model), BF16),
            sds((total, 1), F32),
            sds((total, width), F32),
        ],
        [pltpu.VMEM((MBLK, model), F32)],
        flops=2.2e9,
        moved=10e6,
        prefetch=1,
    )(rank, *merged, *weights, x, gains)


def ffn_kernel(rank_ref, hid_ref, *refs):
    cots = refs[:REL]
    (
        gate_ref,
        down_ref,
        act_out,
        gg_out,
        gu_out,
        cot_out,
        send_out,
        far_out,
        keep_out,
        fsend_out,
        ffar_out,
        fkeep_out,
    ) = refs[REL:]
    step = pl.program_id(0)
    rank = rank_ref[0]
    width = cots[0].shape[1]
    spans = [pl.ds(pl.multiple_of((rank ^ k) * width, width), width) for k in range(REL)]
    for k in range(REL):
        cot_out[:, spans[k]] = cots[k][...]
    hidden = hid_ref[...]
    gate = mm(hidden, gate_ref[0])
    up = mm(hidden, gate_ref[1])
    grad_act = mm(cot_out[...], down_ref[...], NT)
    sig = jax.nn.sigmoid(gate)
    silu = gate * sig
    act = (silu * up).astype(BF16)
    act_out[...] = act
    grad_gate = (grad_act * up * (sig * (1.0 + gate * (1.0 - sig)))).astype(BF16)
    grad_up = (grad_act * silu).astype(BF16)
    gg_out[...] = grad_gate
    gu_out[...] = grad_up
    back = (mm(grad_gate, gate_ref[0], NT) + mm(grad_up, gate_ref[1], NT)).astype(BF16)

    @pl.when(step < 2)
    def _():
        send_out[0] = back

    @pl.when(step == 2)
    def _():
        far_out[0] = back

    @pl.when(step == 3)
    def _():
        keep_out[0] = back

    fkeep_out[...] = mm(act, down_ref[:, spans[0]]).astype(BF16)
    fsend_out[0] = mm(act, down_ref[:, spans[1]]).astype(BF16)
    ffar_out[...] = mm(act, down_ref[:, spans[2]]).astype(BF16)
    fsend_out[1] = mm(act, down_ref[:, spans[3]]).astype(BF16)


def ffn(rank, hidden, cots, gate_up, down):
    total, model = hidden.shape
    units = down.shape[0]
    width = model // REL
    rows = total // REL

    def tok(s, rank_ref):
        g = (s + 1) & 3
        return (rank_ref[0] ^ (g ^ (g >> 1)), 0)

    tok3 = lambda s, r: (0,) + tok(s, r)
    return call(
        ffn_kernel,
        (REL,),
        [pl.BlockSpec((rows, model), tok)]
        + [pl.BlockSpec((rows, width), tok)] * REL
        + [whole(gate_up.shape), whole(down.shape)],
        [pl.BlockSpec((rows, units), tok)] * 3
        + [
            pl.BlockSpec((rows, model), tok),
            pl.BlockSpec((1, rows, model), lambda s, r: (jnp.minimum(s, 1), 0, 0)),
            whole((1, rows, model)),
            whole((1, rows, model)),
            pl.BlockSpec((2, rows, width), tok3),
            pl.BlockSpec((rows, width), tok),
            pl.BlockSpec((rows, width), tok),
        ],
        [sds((total, units), BF16)] * 3
        + [
            sds((total, model), BF16),
            sds((2, rows, model), BF16),
            sds((1, rows, model), BF16),
            sds((1, rows, model), BF16),
            sds((2, total, width), BF16),
            sds((total, width), BF16),
            sds((total, width), BF16),
        ],
        flops=9e9,
        moved=16e6,
        prefetch=1,
    )(rank, hidden, *cots, gate_up, down)


def bend_kernel(rank_ref, keep_ref, near_ref, far_ref, cot_ref, normed_ref, scale_ref, gain_ref, *outs):
    low_out, dgain_out = outs
    grad = (
        keep_ref[0].astype(F32) + near_ref[0].astype(F32) + far_ref[0].astype(F32)
    )
    normed = normed_ref[...].astype(F32)
    dgain_out[...] = jnp.broadcast_to(jnp.sum(grad * normed, 0, keepdims=True), dgain_out.shape)
    g = grad * gain_ref[9:10]
    mean = jnp.mean(g * normed, -1, keepdims=True)
    low_out[...] = (cot_ref[...].astype(F32) + scale_ref[...] * (g - normed * mean)).astype(BF16)


def bend(rank, keep, near, far, cot, normed, scale, gains):
    total, model = cot.shape
    rows = total // REL
    own = lambda s, r: (r[0], 0)
    one = pl.BlockSpec((1, rows, model), lambda *_: (0, 0, 0))
    return call(
        bend_kernel,
        (1,),
        [
            one,
            one,
            one,
            pl.BlockSpec((rows, model), own),
            pl.BlockSpec((rows, model), own),
            pl.BlockSpec((rows, 1), own),
            whole(gains.shape),
        ],
        [whole((rows, model)), whole((8, model))],
        [sds((rows, model), BF16), sds((8, model), F32)],
        flops=5e6,
        moved=4e6,
        prefetch=1,
    )(rank, keep, near, far, cot, normed, scale, gains)


def turn_kernel(rank_ref, *refs, heads):
    lows = refs[:REL]
    (
        w_ref,
        q_ref,
        normed_ref,
        scale_ref,
        aux_ref,
        merged_ref,
        dev_ref,
        ga_out,
        gm_out,
        part_out,
        gout_out,
        share_out,
        load_out,
        low_sc,
        acc_sc,
        state_sc,
    ) = refs[REL:]
    step = pl.program_id(0)
    last = pl.num_programs(0) - 1
    block = last - step
    rank = rank_ref[0]
    rows = q_ref.shape[0]
    scal = 2 * heads * DH
    for k in range(REL):

        @pl.when((rank ^ k) == block)
        def _():
            low_sc[...] = lows[k][...]

    @pl.when(step == 0)
    def _():
        state_sc[...] = jnp.zeros_like(state_sc)
        acc_sc[...] = jnp.zeros_like(acc_sc)

    low = low_sc[...]
    width = share_out.shape[1]
    share_out[...] = low_sc[:, pl.ds(pl.multiple_of(rank * width, width), width)]
    grad_merged = mm(low, w_ref[...], NT)
    ga_out[...] = grad_merged.astype(BF16)
    acc_sc[...] += mm(merged_ref[...], low, TN)
    end = slice(rows - 1, rows)
    for h in range(heads):
        lo, mid = h * DH, (heads + h) * DH
        g = grad_merged[:, lo : lo + DH]
        normed = normed_ref[:, lo : lo + DH]
        scale = scale_ref[:, h : h + 1]
        grad = scale * (g - normed * jnp.mean(g * normed, -1, keepdims=True))
        gm_out[:, lo : lo + DH] = grad.astype(BF16)
        query = q_ref[:, lo : lo + DH]
        keep = aux_ref[:, h : h + 1]
        cross = aux_ref[:, heads + h : heads + h + 1]
        carry = aux_ref[:, 2 * heads + h : 2 * heads + h + 1]
        mem_part = mm((keep * grad).astype(BF16), query, TN)
        mom_part = mm((cross * grad).astype(BF16), query, TN)
        part_out[0, lo : lo + DH] = mem_part
        part_out[0, mid : mid + DH] = mom_part
        memory, momentum = state_sc[lo : lo + DH], state_sc[mid : mid + DH]
        state_sc[lo : lo + DH] = keep[end] * memory + mem_part
        state_sc[mid : mid + DH] = cross[end] * memory + carry[end] * momentum + mom_part

    @pl.when(step == last)
    def _():
        gout_out[...] = acc_sc[...].astype(BF16)
        state_sc[scal : scal + 8] = dev_ref[scal : scal + 8]
        pack_load(load_out, state_sc[...], scal)


def turn(rank, lows, weight, qkv, normed, scales, aux, merged, dev, heads):
    total = qkv.shape[0]
    count = total // MBLK
    local, model = weight.shape
    width = model // REL
    scal = 2 * local
    at = lambda b, *_: (count - 1 - b, 0)
    return call(
        functools.partial(turn_kernel, heads=heads),
        (count,),
        [whole(lows[0].shape)] * REL
        + [
            whole(weight.shape),
            pl.BlockSpec((MBLK, local), at),
            pl.BlockSpec((MBLK, local), at),
            pl.BlockSpec((MBLK, DH), at),
            pl.BlockSpec((MBLK, DH), at),
            pl.BlockSpec((MBLK, local), at),
            whole(dev.shape),
        ],
        [
            pl.BlockSpec((MBLK, local), at),
            pl.BlockSpec((MBLK, local), at),
            pl.BlockSpec((1, scal, DH), lambda b, *_: (count - 1 - b, 0, 0)),
            whole((local, model)),
            pl.BlockSpec((MBLK, width), at),
            whole((scal + 16, DH)),
        ],
        [
            sds((total, local), BF16),
            sds((total, local), BF16),
            sds((count, scal, DH), F32),
            sds((local, model), BF16),
            sds((total, width), BF16),
            sds((scal + 16, DH), BF16),
        ],
        [
            pltpu.VMEM((MBLK, model), BF16),
            pltpu.VMEM((local, model), F32),
            pltpu.VMEM((scal + 8, DH), F32),
        ],
        flops=1.5e9,
        moved=8e6,
        prefetch=1,
    )(rank, *lows, weight, qkv, normed, scales, aux, merged, dev)


def settle_kernel(qkv_ref, *refs, heads):
    atts = refs[: 3 * heads]
    mems = refs[3 * heads : 6 * heads]
    (
        gm_ref,
        aux_ref,
        low_ref,
        part_ref,
        state_ref,
        proj_ref,
        halo_ref,
        conv_ref,
        starts_ref,
        gp_out,
        tail_out,
        head_out,
        gconv_out,
        state_sc,
        mix_sc,
        ext_sc,
        proj_sc,
    ) = refs[6 * heads :]
    step = pl.program_id(0)
    last = pl.num_programs(0) - 1
    block = last - step
    rows = qkv_ref.shape[0]
    local = heads * DH
    base = block * rows

    @pl.when(step == 0)
    def _():
        state_sc[...] = state_ref[0 : state_sc.shape[0]]
        ext_sc[0:8] = jnp.zeros((8, 3 * local), F32)
        gconv_out[...] = jnp.zeros_like(gconv_out)

    end = slice(rows - 1, rows)
    for h in range(heads):
        lo, mid = h * DH, (heads + h) * DH
        memory, momentum = state_sc[lo : lo + DH], state_sc[mid : mid + DH]
        memory_low, momentum_low = memory.astype(BF16), momentum.astype(BF16)
        keep = aux_ref[:, h : h + 1]
        cross = aux_ref[:, heads + h : heads + h + 1]
        carry = aux_ref[:, 2 * heads + h : 2 * heads + h + 1]
        end_kernel = aux_ref[:, 3 * heads + h : 3 * heads + h + 1]
        end_carry = aux_ref[:, 4 * heads + h : 4 * heads + h + 1]
        keys = qkv_ref[:, local + lo : local + lo + DH]
        values = qkv_ref[:, 2 * local + lo : 2 * local + lo + DH]
        gmem = gm_ref[:, lo : lo + DH]
        dq = keep * mm(gmem, low_ref[0, lo : lo + DH]) + cross * mm(
            gmem, low_ref[0, mid : mid + DH]
        )
        dk = end_kernel * mm(values, memory_low) + end_carry * mm(values, momentum_low)
        dv = end_kernel * mm(keys, memory_low, NT) + end_carry * mm(keys, momentum_low, NT)
        for c, extra in enumerate((dq, dk, dv)):
            mix_sc[:, c * local + lo : c * local + lo + DH] = (
                atts[c * heads + h][...] + mems[c * heads + h][...] + extra
            )
        state_sc[lo : lo + DH] = keep[end] * memory + part_ref[0, lo : lo + DH]
        state_sc[mid : mid + DH] = (
            cross[end] * memory + carry[end] * momentum + part_ref[0, mid : mid + DH]
        )
    before = proj_ref[pl.ds(pl.multiple_of(jnp.maximum(base - 16, 0), 16), 16)].astype(F32)[8:16]
    proj_sc[0:8] = jnp.where(block == 0, halo_ref[...], before)
    proj_sc[8 : 8 + rows] = proj_ref[pl.ds(pl.multiple_of(base, rows), rows)].astype(F32)
    ext_sc[rows : rows + 8] = ext_sc[0:8]
    ext_sc[0:rows] = jnp.zeros((rows, 3 * local), F32)
    place = base + iota((rows, 1), 0)
    starts = starts_ref[...]
    for j in range(KW):
        tap = mix_sc[...] * (place - j >= starts).astype(F32)
        ext_sc[8 - j : 8 - j + rows] += conv_ref[j : j + 1] * tap
        gconv_out[j : j + 1] += jnp.sum(tap * proj_sc[8 - j : 8 - j + rows], 0, keepdims=True)
    gp_out[...] = ext_sc[8 : 8 + rows].astype(BF16)

    @pl.when(step == 0)
    def _():
        tail_out[...] = ext_sc[rows - 8 : rows + 8]

    @pl.when(step == last)
    def _():
        head_out[...] = ext_sc[0:8]


def settle(qkv, att_grads, mem_grads, gm, aux, lows, parts, state, proj, halo, conv, starts, heads):
    total = qkv.shape[0]
    count = total // MBLK
    local = heads * DH
    scal = 2 * local
    at = lambda b, *_: (count - 1 - b, 0)
    by_block = pl.BlockSpec((1, scal, DH), lambda b, *_: (count - 1 - b, 0, 0))
    return call(
        functools.partial(settle_kernel, heads=heads),
        (count,),
        [pl.BlockSpec((MBLK, 3 * local), at)]
        + [pl.BlockSpec((MBLK, DH), at)] * (6 * heads)
        + [
            pl.BlockSpec((MBLK, local), at),
            pl.BlockSpec((MBLK, DH), at),
            by_block,
            by_block,
            whole(state.shape),
            whole(proj.shape),
            whole(halo.shape),
            whole(conv.shape),
            pl.BlockSpec((MBLK, 1), at),
        ],
        [
            pl.BlockSpec((MBLK, 3 * local), at),
            whole((16, 3 * local)),
            whole((8, 3 * local)),
            whole((8, 3 * local)),
        ],
        [
            sds((total, 3 * local), BF16),
            sds((16, 3 * local), F32),
            sds((8, 3 * local), F32),
            sds((8, 3 * local), F32),
        ],
        [
            pltpu.VMEM((scal, DH), F32),
            pltpu.VMEM((MBLK, 3 * local), F32),
            pltpu.VMEM((MBLK + 8, 3 * local), F32),
            pltpu.VMEM((MBLK + 8, 3 * local), F32),
        ],
        flops=6e8,
        moved=14e6,
    )(qkv, *att_grads, *mem_grads, gm, aux, lows, parts, state, proj, halo, conv, starts)


def back_kernel(rank_ref, gp_ref, w_ref, x_ref, scale_ref, gain_ref, *outs):
    send_out, far_out, keep_out, dgain_out, grad_sc = outs
    rank = rank_ref[0]
    width = keep_out.shape[1]
    local = w_ref.shape[2]

    @pl.when(pl.program_id(0) == 0)
    def _():
        dgain_out[...] = jnp.zeros_like(dgain_out)

    grad = mm(gp_ref[:, 0:local], w_ref[0], NT)
    for c in range(1, 3):
        grad = grad + mm(gp_ref[:, c * local : (c + 1) * local], w_ref[c], NT)
    scale = scale_ref[...]
    normed = x_ref[...].astype(F32) * scale
    dgain_out[...] += jnp.broadcast_to(jnp.sum(grad * normed, 0, keepdims=True), dgain_out.shape)
    g = grad * gain_ref[8:9]
    grad_sc[...] = (scale * (g - normed * jnp.mean(g * normed, -1, keepdims=True))).astype(BF16)
    spans = [pl.ds(pl.multiple_of((rank ^ k) * width, width), width) for k in range(REL)]
    keep_out[...] = grad_sc[:, spans[0]]
    send_out[0] = grad_sc[:, spans[1]]
    far_out[...] = grad_sc[:, spans[2]]
    send_out[1] = grad_sc[:, spans[3]]


def back(rank, gp, weight, x, scale, gains):
    total, model = x.shape
    width = model // REL
    at = lambda b, *_: (b, 0)
    return call(
        back_kernel,
        (total // MBLK,),
        [
            pl.BlockSpec((MBLK, gp.shape[1]), at),
            whole(weight.shape),
            pl.BlockSpec((MBLK, model), at),
            pl.BlockSpec((MBLK, 1), at),
            whole(gains.shape),
        ],
        [
            pl.BlockSpec((2, MBLK, width), lambda b, *_: (0, b, 0)),
            pl.BlockSpec((MBLK, width), at),
            pl.BlockSpec((MBLK, width), at),
            whole((8, model)),
        ],
        [
            sds((2, total, width), BF16),
            sds((total, width), BF16),
            sds((total, width), BF16),
            sds((8, model), F32),
        ],
        [pltpu.VMEM((MBLK, model), BF16)],
        flops=1.7e9,
        moved=8e6,
        prefetch=1,
    )(rank, gp, weight, x, scale, gains)


def scatter_rel(send, far, keep):
    got = swap(send, "head", 1)
    got_far = swap(far + got[1], "head", 2)
    return keep.astype(F32) + got[0].astype(F32) + got_far.astype(F32)


def per_device(
    inputs,
    cotangent,
    norm_gain,
    qkv_weight,
    conv_kernel,
    persistent,
    out_weight,
    ffn_gain,
    gate_up,
    down_weight,
    memory_decay,
    momentum_decay,
    doc_start,
):
    total, width = inputs.shape
    local = qkv_weight.shape[2]
    heads = local // DH
    model = width * REL
    rank = lax.axis_index("head").astype(jnp.int32).reshape(1)
    starts = (doc_start - lax.axis_index("seq") * total).reshape(total, 1)
    decays = jnp.concatenate(
        [memory_decay.T, momentum_decay.T, jnp.ones((8 - 2 * heads, total), F32)], 0
    )
    conv = conv_kernel.reshape(KW, 3 * local)

    halo_rows = shifted(inputs[total - 8 :], "seq", 1)
    small = jnp.concatenate(
        [halo_rows, norm_gain[None], ffn_gain[None], jnp.zeros((6, width), BF16)], 0
    )
    blocks = gather_rel(inputs)
    smalls = gather_rel(small)
    cots = gather_rel(cotangent)
    out_weights = gather_rel(out_weight)

    (
        x,
        hidden_one,
        scale_one,
        proj,
        qkv,
        kmat,
        aux,
        parts,
        halo,
        gains,
        dev_state,
        load,
    ) = front(rank, blocks, smalls, qkv_weight, conv, starts, decays, heads)

    atts, ratios, intras, probs, fixps = zip(
        *[attend(qkv, persistent, starts, kmat, h, heads) for h in range(heads)]
    )
    prefix = entering(load, heads, False)
    merged, normed_mem, mem_scales, state_lows = merge(
        qkv, atts, intras, aux, parts, prefix, heads
    )
    merged_rel = gather_rel(merged)
    hidden_two, normed_two, scale_two, middle_share = middle(
        rank, merged_rel, out_weights, x, gains
    )
    act, grad_gate, grad_up, cot, send, far, keep, fsend, ffar, fkeep = ffn(
        rank, hidden_two, cots, gate_up, down_weight
    )
    near = swap(send, "head", 1)
    far_sum = swap(far + near[1:2], "head", 2)
    low_own, dgain_two = bend(rank, keep, near, far_sum, cot, normed_two, scale_two, gains)
    lows = gather_rel(low_own)

    output = (middle_share + scatter_rel(fsend, ffar, fkeep)).astype(BF16)
    grad_down = lax.dot_general(act, cot, TN, preferred_element_type=F32).astype(BF16)
    grad_gate_full = lax.dot_general(
        hidden_two, grad_gate, TN, preferred_element_type=F32
    ).astype(BF16)
    grad_up_full = lax.dot_general(hidden_two, grad_up, TN, preferred_element_type=F32).astype(
        BF16
    )

    grad_att, grad_mem, mem_parts, grad_out, low_share, back_load = turn(
        rank, lows, out_weight, qkv, normed_mem, mem_scales, aux, merged, dev_state, heads
    )
    pieces = [
        attend_back(
            qkv, persistent, probs[h], fixps[h], ratios[h], grad_att, grad_mem, kmat, h, heads
        )
        for h in range(heads)
    ]
    suffix = entering(back_load, heads, True)
    att_grads = [pieces[h][c] for c in range(3) for h in range(heads)]
    mem_grads = [pieces[h][4 + c] for c in range(3) for h in range(heads)]
    gp, tail, head_rows, gconv = settle(
        qkv,
        att_grads,
        mem_grads,
        grad_mem,
        aux,
        state_lows,
        mem_parts,
        suffix,
        proj,
        halo,
        conv,
        starts,
        heads,
    )
    returned = shifted(head_rows, "seq", -1)
    fixed_tail = jnp.concatenate([tail[:8], tail[8:] + returned], 0).astype(BF16)
    gp = lax.dynamic_update_slice(gp, fixed_tail, (total - 16, 0))
    bsend, bfar, bkeep, dgain_one = back(rank, gp, qkv_weight, x, scale_one, gains)
    grad_qkv = jnp.stack(
        [
            lax.dot_general(
                hidden_one,
                gp[:, c * local : (c + 1) * local],
                TN,
                preferred_element_type=F32,
            ).astype(BF16)
            for c in range(3)
        ],
        0,
    )
    input_grad = scatter_rel(bsend, bfar, bkeep) + low_share.astype(F32)

    grad_fixed = jnp.concatenate([p[3] for p in pieces], -1)
    gain_sums = sum_over(jnp.stack([dgain_one[0], dgain_two[0]], 0), "head")
    gain_own = lax.dynamic_slice_in_dim(
        gain_sums, lax.axis_index("head") * width, width, 1
    )
    fixed_count = persistent.shape[1]
    little = jnp.concatenate(
        [
            gain_own,
            gconv[:KW].reshape(3 * KW, local),
            grad_fixed.reshape(2 * fixed_count, local),
        ],
        0,
    )
    little = sum_over(little, "seq")
    scatter = lambda g, dim: lax.psum_scatter(
        g, "seq", scatter_dimension=dim, tiled=True
    ).astype(F32)
    return (
        output,
        input_grad,
        little[0],
        scatter(grad_qkv, 1),
        little[2 : 2 + 3 * KW].reshape(KW, 3, local),
        little[2 + 3 * KW :].reshape(2, fixed_count, local),
        scatter(grad_out, 1),
        little[1],
        scatter(jnp.stack([grad_gate_full, grad_up_full], 0), 1),
        scatter(grad_down, 1),
    )


def solution(mesh):
    placed = (
        P("seq", "head"),
        P("seq", "head"),
        P("head"),
        P(None, None, "head"),
        P(None, None, "head"),
        P(None, None, "head"),
        P("head", None),
        P("head"),
        P(None, None, "head"),
        P("head", None),
        P("seq", "head"),
        P("seq", "head"),
        P("seq"),
    )
    return jax.shard_map(
        per_device,
        mesh=mesh,
        in_specs=placed,
        out_specs=(
            P("seq", "head"),
            P("seq", "head"),
            P("head"),
            P(None, "seq", "head"),
            P(None, None, "head"),
            P(None, None, "head"),
            P("head", "seq"),
            P("head"),
            P(None, "seq", "head"),
            P("head", "seq"),
        ),
        check_vma=False,
    )
```

time: 1150 us -> 438 us (0.38)
  waiting for transfers between devices: 413 us -> 191 us
  blocking collectives: 204 us -> 0 us
  matrix products: 194 us -> 12.1 us
  local copies, waits for them, and re-layouts: 197 us -> 36.5 us
  Pallas kernels: 0 us -> 113 us
  other arithmetic: 110 us -> 14.3 us
  starting transfers between devices: 5.47 us -> 49.1 us
    reduce_scatter x6 -> x1, waiting for transfers between devices: 280 us -> 65.1 us  [per_device(): lax.psum_scatter(g, 'seq', scatter_dimension=dim, tiled=True).astype(F32)]
    dot_general x116 -> x6, matrix products: 194 us -> 12.1 us  [the longest x1 3.76 us: per_device(): lax.dot_general(act, cot, TN, preferred_element_type=F32).astype(BF16)]
    all_gather x6 -> x0, blocking collectives: 141 us -> none  [the longest x4 130 us: entering(): lax.all_gather(a.astype(kind), axis)]
    pallas_call x0 -> x18, Pallas kernels: none -> 113 us  [the longest x1 19.7 us: ffn(): call(ffn_kernel, (REL,), [pl.BlockSpec((rows, model), tok)] + [pl.BlockSp...]
    psum x2 -> x0, waiting for transfers between devices: 94.9 us -> none  [the longest x1 48.6 us: per_device(): lax.psum(mixer_part.astype(jnp.bfloat16), 'head').astype(jnp.float32)]
    ppermute x2 -> x39, waiting for transfers between devices: 5.53 us -> 87.1 us  [the longest x29 71.7 us: swap(): return lax.ppermute(x, axis, [(i, i ^ bit) for i in range(count)])]
    dynamic_update_slice x8 -> x0, local copies, waits for them, and re-layouts: 46.2 us -> none  [per_device(): lax.map(forward_block, (query_blocks, row_blocks, start_blocks))]
    ppermute x2 -> x39, starting transfers between devices: 4.85 us -> 48.7 us  [the longest x10 26.9 us: shifted(): lax.ppermute(x, axis, [(i, i + by) for i in range(count) if 0 <= i + by <...]
  transfers between devices with their start and end apart: 12 -> 43, of which waited for: 9 -> 20; matrix products, arithmetic and copies ran while one was open for 24% -> 12% of each run, Pallas kernels for 0% -> 18%
where the time goes in v1:
time: 438 us; the launch traced here: 431 us
  waiting for transfers between devices  191 us (44%)
  Pallas kernels  113 us (26%)
  starting transfers between devices  49.1 us (11%)
  local copies, waits for them, and re-layouts  36.5 us (8%)
  between operations  14.8 us (3%)
  other arithmetic  14.3 us (3%)
  matrix products  12.1 us (3%)
    ppermute x29, waiting for transfers between devices, swap(): return lax.ppermute(x, axis, [(i, i ^ bit) for i in range(count)])  71.7 us
    reduce_scatter x1, waiting for transfers between devices, per_device(): lax.psum_scatter(g, 'seq', scatter_dimension=dim, tiled=True).astype(F32)  65.1 us
    unnamed x7, waiting for transfers between devices  38.6 us
    unnamed x88, local copies, waits for them, and re-layouts  29.7 us
    ppermute x10, starting transfers between devices, shifted(): lax.ppermute(x, axis, [(i, i + by) for i in range(count) if 0 <= i + by <...  26.9 us
    ppermute x29, starting transfers between devices, swap(): return lax.ppermute(x, axis, [(i, i ^ bit) for i in range(count)])  21.8 us
    pallas_call x1, Pallas kernels, ffn(): call(ffn_kernel, (REL,), [pl.BlockSpec((rows, model), tok)] + [pl.BlockSp...  19.7 us
    ppermute x10, waiting for transfers between devices, shifted(): lax.ppermute(x, axis, [(i, i + by) for i in range(count) if 0 <= i + by <...  15.4 us
  transfers between devices with their start and end apart: 43, of which 20 were waited for; matrix products, arithmetic and copies ran while one was open for 12% of the time, Pallas kernels for 18%

profile of v1, /device:TPU:0, one launch (start us, length us, event | category | flops | bytes accessed | tf_op | source)
XLA Modules:
  0.0 431.0 jit_solution(11762540563611882203)
XLA Ops:
  7.2 3.0 collective-permute-start.1
  10.9 3.4 collective-permute-start.3
  15.9 6.4 %collective-permute-done.1.refs_2_ = bf16[1024,256]{1,0:T(8,128)(2,1)S(1)} collective-permute-done((bf16[1024,256]{1,0:T(8,128)(2,1)}, bf16[1024,256]{1,0:T(8,128)(2,1)S(1)}, u32[]{:S(2)}, u32[]{:S(2)}) %collective-permute-start.1) | collective-permute-done | bytes 524320 | tf_op jit(solution)/shard_map/ppermute | solution.py:68
  28.9 15.1 %shard_map.204 = (bf16[1024,1024]{1,0:T(8,128)(2,1)}, bf16[1024,1024]{1,0:T(8,128)(2,1)}, f32[1024,1]{1,0:T(8,128)}, bf16[1024,768]{1,0:T(8,128)(2,1)}, bf16[102...) custom-call(s32[1]{0:T(128)} %bitcast.rank_ref, ...), custom_call_target="tpu_custom_call" | custom-call | flops 2200000000 | bytes 12000000 | tf_op jit(solution)/shard_map/pallas_call | solution.py:238
  44.0 3.7 collective-permute-start.7
  47.7 3.4 collective-permute-start.8
  52.7 1.9 collective-permute-done.8.second_ref
  57.1 5.3 %collective-permute-start.9 = (bf16[528,128]{1,0:T(8,128)(2,1)}, bf16[528,128]{1,0:T(8,128)(2,1)S(1)}, u32[]{:S(2)}, u32[]{:S(2)}) collective-permute-start(bf16[528,128]{1,0:T(8,128)(2,1)} %get-tuple-element.99), channel_id=1, source_target_pairs={{0,8},{4,12},{8,16},{12,20},{16,24},{20,28},{1,9},{5,13},{9,17},{1... | collective-permute-start | bytes 405512 | tf_op jit(solution)/shard_map/ppermute | solution.py:73
  62.4 6.2 %shard_map.206 = (f32[1024,128]{1,0:T(8,128)}, f32[1024,128]{1,0:T(8,128)}, f32[1024,128]{1,0:T(8,128)}, bf16[1024,1024]{1,0:T(8,128)(2,1)}, bf16[1024,16]{1,0:T(8,128)(2,1)}) custom-call(bf16[1024,768]{1,0:T(8,128)(2,1)} %get-tuple-element.90.q_ref.k_ref.v_ref.refs_5_.qkv_ref, bf16[1024,768]{1,0:T(8,128)(2,1)} %get-tuple-element.90.q_ref.k_ref.v_ref.refs_5_.qkv_ref, ...), custom_call_target="tpu_custom_call" | custom-call | flops 1500000000 | bytes 8000000 | tf_op jit(solution)/shard_map/pallas_call | solution.py:388
  69.2 1.9 shard_map.208
  71.1 4.4 %collective-permute-start.10 = (bf16[528,128]{1,0:T(8,128)(2,1)}, bf16[528,128]{1,0:T(8,128)(2,1)S(1)}, u32[]{:S(2)}, u32[]{:S(2)}) collective-permute-start(bf16[528,128]{1,0:T(8,128)(2,1)} %get-tuple-element.101), channel_id=1, source_target_pairs={{0,16},{4,20},{8,24},{12,28},{1,17},{5,21},{9,25},{13,29},{2,18},{... | collective-permute-start | bytes 405512 | tf_op jit(solution)/shard_map/ppermute | solution.py:73
  75.5 6.1 %shard_map.205 = (f32[1024,128]{1,0:T(8,128)}, f32[1024,128]{1,0:T(8,128)}, f32[1024,128]{1,0:T(8,128)}, bf16[1024,1024]{1,0:T(8,128)(2,1)}, bf16[1024,16]{1,0:T(8,128)(2,1)}) custom-call(bf16[1024,768]{1,0:T(8,128)(2,1)} %get-tuple-element.90.q_ref.k_ref.v_ref.refs_5_.qkv_ref, bf16[1024,768]{1,0:T(8,128)(2,1)} %get-tuple-element.90.q_ref.k_ref.v_ref.refs_5_.qkv_ref, ...), custom_call_target="tpu_custom_call" | custom-call | flops 1500000000 | bytes 8000000 | tf_op jit(solution)/shard_map/pallas_call | solution.py:388
  82.3 1.8 shard_map.209
  84.1 5.6 %shard_map.210 = (bf16[1024,256]{1,0:T(8,128)(2,1)}, f32[1024,256]{1,0:T(8,128)}, f32[1024,128]{1,0:T(8,128)}, bf16[4,512,128]{2,1,0:T(8,128)(2,1)}) custom-call(bf16[1024,768]{1,0:T(8,128)(2,1)} %get-tuple-element.90.q_ref.k_ref.v_ref.refs_5_.qkv_ref, f32[1024,128]{1,0:T(8,128)} %get-tuple-element.92.refs_0_, f32[1024,128]{1,0:T(8,128)} %get-tuple-element.93.refs_1_, ...), custom_call_target="tpu_custom_call" | custom-call | flops 300000000 | bytes 6000000 | tf_op jit(solution)/shard_map/pallas_call | solution.py:524
  92.3 12.6 %collective-permute-done.12.refs_2_ = bf16[1024,256]{1,0:T(8,128)(2,1)} collective-permute-done((bf16[1024,256]{1,0:T(8,128)(2,1)}, bf16[1024,256]{1,0:T(8,128)(2,1)}, u32[]{:S(2)}, u32[]{:S(2)}) %collective-permute-start.12) | collective-permute-done | bytes 524320 | tf_op jit(solution)/shard_map/ppermute | solution.py:68
  105.5 8.9 %collective-permute-done.18.refs_2_ = bf16[1024,256]{1,0:T(8,128)(2,1)} collective-permute-done((bf16[1024,256]{1,0:T(8,128)(2,1)S(1)}, bf16[1024,256]{1,0:T(8,128)(2,1)}, u32[]{:S(2)}, u32[]{:S(2)}) %collective-permute-start.18) | collective-permute-done | bytes 524320 | tf_op jit(solution)/shard_map/ppermute | solution.py:68
  114.4 2.8 copy.34.refs_4_
  117.2 7.6 %shard_map.211 = (bf16[1024,1024]{1,0:T(8,128)(2,1)}, bf16[1024,1024]{1,0:T(8,128)(2,1)}, f32[1024,1]{1,0:T(8,128)}, f32[1024,256]{1,0:T(8,128)}) custom-call(s32[1]{0:T(128)} %bitcast.rank_ref, bf16[1024,256]{1,0:T(8,128)(2,1)} %get-tuple-element.104.refs_0_.refs_9_, bf16[1024,256]{1,0:T(8,128)(2,1)} %collective-permute-done.11.refs_1_, ...), custom_call_target="tpu_custom_call" | custom-call | flops 2200000000 | bytes 10000000 | tf_op jit(solution)/shard_map/pallas_call | solution.py:569
  124.8 19.7 %shard_map.212 = (bf16[1024,704]{1,0:T(8,128)(2,1)}, bf16[1024,704]{1,0:T(8,128)(2,1)}, bf16[1024,704]{1,0:T(8,128)(2,1)}, bf16[1024,1024]{1,0:T(8,128)(2,1)}, b...) custom-call(s32[1]{0:T(128)} %bitcast.rank_ref, ...), custom_call_target="tpu_custom_call" | custom-call | flops 8999999488 | bytes 16000000 | tf_op jit(solution)/shard_map/pallas_call | solution.py:659
  145.1 3.8 convolution_convert_fusion
  152.3 12.4 %collective-permute-done.23.far_ref = bf16[1,256,1024]{2,1,0:T(8,128)(2,1)S(1)} collective-permute-done((bf16[1,256,1024]{2,1,0:T(8,128)(2,1)S(1)}, bf16[1,256,1024]{2,1,0:T(8,128)(2,1)S(1)}, u32[]{:S(2)}, u32[]{:S(2)}) %collective-permute-start.23) | collective-permute-done | bytes 524320 | tf_op jit(solution)/shard_map/ppermute | solution.py:68
  165.5 3.2 shard_map.213
  170.2 11.9 %collective-permute-done.25.refs_2_ = bf16[256,1024]{1,0:T(8,128)(2,1)S(1)} collective-permute-done((bf16[256,1024]{1,0:T(8,128)(2,1)}, bf16[256,1024]{1,0:T(8,128)(2,1)S(1)}, u32[]{:S(2)}, u32[]{:S(2)}) %collective-permute-start.25) | collective-permute-done | bytes 524320 | tf_op jit(solution)/shard_map/ppermute | solution.py:68
  182.1 1.9 collective-permute-done.26.refs_3_
  184.8 7.7 %shard_map.214 = (bf16[1024,256]{1,0:T(8,128)(2,1)}, bf16[1024,256]{1,0:T(8,128)(2,1)}, f32[4,512,128]{2,1,0:T(8,128)}, bf16[256,1024]{1,0:T(8,128)(2,1)}, bf16[...) custom-call(s32[1]{0:T(128)} %bitcast.rank_ref, bf16[256,1024]{1,0:T(8,128)(2,1)} %get-tuple-element.121.refs_0_, ...), custom_call_target="tpu_custom_call" | custom-call | flops 1500000000 | bytes 8000000 | tf_op jit(solution)/shard_map/pallas_call | solution.py:805
  192.5 2.0 copy.37
  194.7 3.2 fusion
  199.6 1.8 pad_maximum_fusion
  201.5 7.6 %copy.39 = bf16[2,1024,704]{2,0,1:T(2,128)(2,1)S(1)} copy(bf16[2,1024,704]{1,2,0:T(8,128)(2,1)} %pad_maximum_fusion) | data formatting | bytes 5767168
  209.1 3.4 reshape.56
  216.0 5.7 %collective-permute-done.27.first_ref = bf16[528,128]{1,0:T(8,128)(2,1)S(1)} collective-permute-done((bf16[528,128]{1,0:T(8,128)(2,1)S(1)}, bf16[528,128]{1,0:T(8,128)(2,1)S(1)}, u32[]{:S(2)}, u32[]{:S(2)}) %collective-permute-start.27) | collective-permute-done | bytes 135200 | tf_op jit(solution)/shard_map/ppermute | solution.py:73
  226.1 7.2 %shard_map.216 = (f32[1024,128]{1,0:T(8,128)}, f32[1024,128]{1,0:T(8,128)}, f32[1024,128]{1,0:T(8,128)}, f32[2,16,128]{2,1,0:T(8,128)}, f32[1024,128]{1,0:T(8,12...) custom-call(bf16[1024,768]{1,0:T(8,128)(2,1)} %get-tuple-element.90.q_ref.k_ref.v_ref.refs_5_.qkv_ref, ...), custom_call_target="tpu_custom_call" | custom-call | flops 3000000000 | bytes 10000000 | tf_op jit(solution)/shard_map/pallas_call | solution.py:452
  234.0 1.8 shard_map.218
  237.3 7.1 %shard_map.215 = (f32[1024,128]{1,0:T(8,128)}, f32[1024,128]{1,0:T(8,128)}, f32[1024,128]{1,0:T(8,128)}, f32[2,16,128]{2,1,0:T(8,128)}, f32[1024,128]{1,0:T(8,12...) custom-call(bf16[1024,768]{1,0:T(8,128)(2,1)} %get-tuple-element.90.q_ref.k_ref.v_ref.refs_5_.qkv_ref, ...), custom_call_target="tpu_custom_call" | custom-call | flops 3000000000 | bytes 10000000 | tf_op jit(solution)/shard_map/pallas_call | solution.py:452
  244.4 3.0 collective-permute-done.30.first_ref
  248.1 1.8 shard_map.219
  249.9 10.0 %shard_map.220 = (bf16[1024,768]{1,0:T(8,128)(2,1)}, f32[16,768]{1,0:T(8,128)}, f32[8,768]{1,0:T(8,128)}, f32[8,768]{1,0:T(8,128)}) custom-call(bf16[1024,768]{1,0:T(8,128)(2,1)} %get-tuple-element.90.q_ref.k_ref.v_ref.refs_5_.qkv_ref, f32[1024,128]{1,0:T(8,128)} %get-tuple-element.127.refs_0_, f32[1024,128]{1,0:T(8,128)} %get-tuple-element.131.refs_1_, ...), custom_call_target="tpu_custom_call" | custom-call | flops 600000000 | bytes 14000000 | tf_op jit(solution)/shard_map/pallas_call | solution.py:935
  262.0 4.3 collective-permute-done.31
  267.6 1.9 fusion.2
  273.2 7.0 %shard_map.221 = (bf16[2,1024,256]{2,1,0:T(8,128)(2,1)}, bf16[1024,256]{1,0:T(8,128)(2,1)}, bf16[1024,256]{1,0:T(8,128)(2,1)}, f32[8,1024]{1,0:T(8,128)}) custom-call(s32[1]{0:T(128)} %bitcast.rank_ref, bf16[1024,768]{1,0:T(8,128)(2,1)} %maximum_dynamic-update-slice_fusion.gp_ref, bf16[3,1024,256]{2,1,0:T(8,128)(2,1)} %w_ref.1, ...), custom_call_target="tpu_custom_call" | custom-call | flops 1700000000 | bytes 8000000 | tf_op jit(solution)/shard_map/pallas_call | solution.py:1003
  284.1 2.1 collective-permute-done.35
  286.2 3.0 collective-permute-start.36
  292.4 6.5 %collective-permute-done.37 = f32[46,256]{1,0:T(8,128)S(1)} collective-permute-done((f32[46,256]{1,0:T(8,128)S(1)}, f32[46,256]{1,0:T(8,128)S(1)}, u32[]{:S(2)}, u32[]{:S(2)}) %collective-permute-start.37) | collective-permute-done | bytes 47136 | tf_op jit(solution)/shard_map/ppermute | solution.py:68
  300.6 3.7 collective-permute-done.21
  310.8 2.8 collective-permute-done.33
  313.5 2.3 fusion.6
  315.8 38.5 %reduce-scatter.15.cloned.1.call-done = bf16[128,1408]{1,0:T(8,128)(2,1)} async-done(((bf16[1024,1408]{1,0:T(8,128)(2,1)}), bf16[128,1408]{1,0:T(8,128)(2,1)}) %reduce-scatter.15.cloned.1.call-update) | async-done | bytes 360464
  357.2 65.1 %reduce-scatter.11.cloned.1.call-done = bf16[3,128,256]{2,1,0:T(8,128)(2,1)} async-done(((bf16[3,1024,256]{2,1,0:T(8,128)(2,1)}), bf16[3,128,256]{2,1,0:T(8,128)(2,1)}) %reduce-scatter.11.cloned.1.call-update) | async-done | bytes 196624 | tf_op jit(solution)/shard_map/reduce_scatter | solution.py:1176
  (195 shorter events, 63.5 us)
Async XLA Ops:
  7.2 298.2 %reduce-scatter.17.cloned.1.call-start = ((), (), s32[]{:S(2)}) async-start(), calls=%async_computation.7 | async-start | bytes 1769472
  7.2 15.1 %collective-permute-start.1 = (bf16[1024,256]{1,0:T(8,128)(2,1)}, bf16[1024,256]{1,0:T(8,128)(2,1)S(1)}, u32[]{:S(2)}, u32[]{:S(2)}) collective-permute-start(bf16[1024,256]{1,0:T(8,128)(2,1)} %refs_0_.2), channel_id=1, source_target_pairs={{0,2},{1,3},{2,0},{3,1},{4,6},{5,7},{6,4},{7,5},{8,10},{9,11},{10,... | collective-permute-start | bytes 1572872 | tf_op jit(solution)/shard_map/ppermute | solution.py:68
  10.9 11.4 %collective-permute-start.3 = (bf16[8,256]{1,0:T(8,128)(2,1)S(1)}, bf16[8,256]{1,0:T(8,128)(2,1)S(1)}, u32[]{:S(2)}, u32[]{:S(2)}) collective-permute-start(bf16[8,256]{1,0:T(8,128)(2,1)S(1)} %slice.55), channel_id=1, source_target_pairs={{0,4},{4,8},{8,12},{12,16},{16,20},{20,24},{24,28},{1,5},{5,9},{9,... | collective-permute-start | bytes 12296 | tf_op jit(solution)/shard_map/ppermute | solution.py:73
  14.4 13.5 %collective-permute-start = (bf16[1024,256]{1,0:T(8,128)(2,1)}, bf16[1024,256]{1,0:T(8,128)(2,1)S(1)}, u32[]{:S(2)}, u32[]{:S(2)}) collective-permute-start(bf16[1024,256]{1,0:T(8,128)(2,1)} %refs_0_.2), channel_id=1, source_target_pairs={{0,1},{1,0},{2,3},{3,2},{4,5},{5,4},{6,7},{7,6},{8,9},{9,8},{10,11... | collective-permute-start | bytes 1572872 | tf_op jit(solution)/shard_map/ppermute | solution.py:68
  22.4 5.6 %collective-permute-start.2 = (bf16[1024,256]{1,0:T(8,128)(2,1)S(1)}, bf16[1024,256]{1,0:T(8,128)(2,1)S(1)}, u32[]{:S(2)}, u32[]{:S(2)}) collective-permute-start(bf16[1024,256]{1,0:T(8,128)(2,1)S(1)} %collective-permute-done.1.refs_2_), channel_id=1, source_target_pairs={{0,1},{1,0},{2,3},{3,2},{4,5},{5,4},{6,7},{7,6},{8,9},{9,8},{10,11... | collective-permute-start | bytes 1572872 | tf_op jit(solution)/shard_map/ppermute | solution.py:68
  22.5 3.7 collective-permute-start.5
  25.6 2.3 collective-permute-start.4
  26.1 1.8 collective-permute-start.6
  28.9 22.3 %copy-start.3 = (bf16[256,1024]{1,0:T(8,128)(2,1)S(1)}, bf16[256,1024]{1,0:T(8,128)(2,1)}, u32[]{:S(2)}) copy-start(bf16[256,1024]{1,0:T(8,128)(2,1)} %refs_4_.4) | copy-start | bytes 1572868
  44.0 8.8 %collective-permute-start.7 = (bf16[528,128]{1,0:T(8,128)(2,1)}, bf16[528,128]{1,0:T(8,128)(2,1)S(1)}, u32[]{:S(2)}, u32[]{:S(2)}) collective-permute-start(bf16[528,128]{1,0:T(8,128)(2,1)} %get-tuple-element.98), channel_id=1, source_target_pairs={{0,8},{4,12},{8,16},{12,20},{16,24},{20,28},{1,9},{5,13},{9,17},{1... | collective-permute-start | bytes 405512 | tf_op jit(solution)/shard_map/ppermute | solution.py:73
  47.7 6.9 %collective-permute-start.8 = (bf16[528,128]{1,0:T(8,128)(2,1)}, bf16[528,128]{1,0:T(8,128)(2,1)S(1)}, u32[]{:S(2)}, u32[]{:S(2)}) collective-permute-start(bf16[528,128]{1,0:T(8,128)(2,1)} %get-tuple-element.98), channel_id=1, source_target_pairs={{0,4},{4,8},{8,12},{12,16},{16,20},{20,24},{24,28},{1,5},{5,9},{9,... | collective-permute-start | bytes 405512 | tf_op jit(solution)/shard_map/ppermute | solution.py:73
  51.2 40.7 %collective-permute-start.15 = (bf16[256,1024]{1,0:T(8,128)(2,1)S(1)}, bf16[256,1024]{1,0:T(8,128)(2,1)}, u32[]{:S(2)}, u32[]{:S(2)}) collective-permute-start(bf16[256,1024]{1,0:T(8,128)(2,1)S(1)} %copy-done.3), channel_id=1, source_target_pairs={{0,2},{1,3},{2,0},{3,1},{4,6},{5,7},{6,4},{7,5},{8,10},{9,11},{10,... | collective-permute-start | bytes 1572872 | tf_op jit(solution)/shard_map/ppermute | solution.py:68
  57.1 11.5 %collective-permute-start.9 = (bf16[528,128]{1,0:T(8,128)(2,1)}, bf16[528,128]{1,0:T(8,128)(2,1)S(1)}, u32[]{:S(2)}, u32[]{:S(2)}) collective-permute-start(bf16[528,128]{1,0:T(8,128)(2,1)} %get-tuple-element.99), channel_id=1, source_target_pairs={{0,8},{4,12},{8,16},{12,20},{16,24},{20,28},{1,9},{5,13},{9,17},{1... | collective-permute-start | bytes 405512 | tf_op jit(solution)/shard_map/ppermute | solution.py:73
  71.1 10.6 %collective-permute-start.10 = (bf16[528,128]{1,0:T(8,128)(2,1)}, bf16[528,128]{1,0:T(8,128)(2,1)S(1)}, u32[]{:S(2)}, u32[]{:S(2)}) collective-permute-start(bf16[528,128]{1,0:T(8,128)(2,1)} %get-tuple-element.101), channel_id=1, source_target_pairs={{0,16},{4,20},{8,24},{12,28},{1,17},{5,21},{9,25},{13,29},{2,18},{... | collective-permute-start | bytes 405512 | tf_op jit(solution)/shard_map/ppermute | solution.py:73
  84.1 30.3 %copy-start = (bf16[2,1024,704]{1,2,0:T(8,128)(2,1)S(1)}, bf16[2,1024,704]{1,2,0:T(8,128)(2,1)}, u32[]{:S(2)}) copy-start(bf16[2,1024,704]{1,2,0:T(8,128)(2,1)} %param.21) | copy-start | bytes 8650756
  89.7 15.2 %collective-permute-start.12 = (bf16[1024,256]{1,0:T(8,128)(2,1)}, bf16[1024,256]{1,0:T(8,128)(2,1)}, u32[]{:S(2)}, u32[]{:S(2)}) collective-permute-start(bf16[1024,256]{1,0:T(8,128)(2,1)} %get-tuple-element.104.refs_0_.refs_9_), channel_id=1, source_target_pairs={{0,2},{1,3},{2,0},{3,1},{4,6},{5,7},{6,4},{7,5},{8,10},{9,11},{10,... | collective-permute-start | bytes 1572872 | tf_op jit(solution)/shard_map/ppermute | solution.py:68
  91.3 13.7 %collective-permute-start.14 = (bf16[256,1024]{1,0:T(8,128)(2,1)S(1)}, bf16[256,1024]{1,0:T(8,128)(2,1)S(1)}, u32[]{:S(2)}, u32[]{:S(2)}) collective-permute-start(bf16[256,1024]{1,0:T(8,128)(2,1)S(1)} %copy-done.3), channel_id=1, source_target_pairs={{0,1},{1,0},{2,3},{3,2},{4,5},{5,4},{6,7},{7,6},{8,9},{9,8},{10,11... | collective-permute-start | bytes 1572872 | tf_op jit(solution)/shard_map/ppermute | solution.py:68
  91.3 23.1 %collective-permute-start.18 = (bf16[1024,256]{1,0:T(8,128)(2,1)S(1)}, bf16[1024,256]{1,0:T(8,128)(2,1)}, u32[]{:S(2)}, u32[]{:S(2)}) collective-permute-start(bf16[1024,256]{1,0:T(8,128)(2,1)S(1)} %copy-done.27), channel_id=1, source_target_pairs={{0,2},{1,3},{2,0},{3,1},{4,6},{5,7},{6,4},{7,5},{8,10},{9,11},{10,... | collective-permute-start | bytes 1572872 | tf_op jit(solution)/shard_map/ppermute | solution.py:68
  91.8 25.3 %collective-permute-start.16 = (bf16[256,1024]{1,0:T(8,128)(2,1)}, bf16[256,1024]{1,0:T(8,128)(2,1)}, u32[]{:S(2)}, u32[]{:S(2)}) collective-permute-start(bf16[256,1024]{1,0:T(8,128)(2,1)} %collective-permute-done.15.refs_6_), channel_id=1, source_target_pairs={{0,1},{1,0},{2,3},{3,2},{4,5},{5,4},{6,7},{7,6},{8,9},{9,8},{10,11... | collective-permute-start | bytes 1572872 | tf_op jit(solution)/shard_map/ppermute | solution.py:68
  92.1 25.1 %collective-permute-start.11 = (bf16[1024,256]{1,0:T(8,128)(2,1)}, bf16[1024,256]{1,0:T(8,128)(2,1)}, u32[]{:S(2)}, u32[]{:S(2)}) collective-permute-start(bf16[1024,256]{1,0:T(8,128)(2,1)} %get-tuple-element.104.refs_0_.refs_9_), channel_id=1, source_target_pairs={{0,1},{1,0},{2,3},{3,2},{4,5},{5,4},{6,7},{7,6},{8,9},{9,8},{10,11... | collective-permute-start | bytes 1572872 | tf_op jit(solution)/shard_map/ppermute | solution.py:68
  105.0 12.2 %collective-permute-start.13 = (bf16[1024,256]{1,0:T(8,128)(2,1)}, bf16[1024,256]{1,0:T(8,128)(2,1)}, u32[]{:S(2)}, u32[]{:S(2)}) collective-permute-start(bf16[1024,256]{1,0:T(8,128)(2,1)} %collective-permute-done.12.refs_2_), channel_id=1, source_target_pairs={{0,1},{1,0},{2,3},{3,2},{4,5},{5,4},{6,7},{7,6},{8,9},{9,8},{10,11... | collective-permute-start | bytes 1572872 | tf_op jit(solution)/shard_map/ppermute | solution.py:68
  105.0 19.8 %collective-permute-start.17 = (bf16[1024,256]{1,0:T(8,128)(2,1)S(1)}, bf16[1024,256]{1,0:T(8,128)(2,1)}, u32[]{:S(2)}, u32[]{:S(2)}) collective-permute-start(bf16[1024,256]{1,0:T(8,128)(2,1)S(1)} %copy-done.27), channel_id=1, source_target_pairs={{0,1},{1,0},{2,3},{3,2},{4,5},{5,4},{6,7},{7,6},{8,9},{9,8},{10,11... | collective-permute-start | bytes 1572872 | tf_op jit(solution)/shard_map/ppermute | solution.py:68
  114.4 10.5 %collective-permute-start.19 = (bf16[1024,256]{1,0:T(8,128)(2,1)}, bf16[1024,256]{1,0:T(8,128)(2,1)}, u32[]{:S(2)}, u32[]{:S(2)}) collective-permute-start(bf16[1024,256]{1,0:T(8,128)(2,1)} %collective-permute-done.18.refs_2_), channel_id=1, source_target_pairs={{0,1},{1,0},{2,3},{3,2},{4,5},{5,4},{6,7},{7,6},{8,9},{9,8},{10,11... | collective-permute-start | bytes 1572872 | tf_op jit(solution)/shard_map/ppermute | solution.py:68
  144.5 6.2 %collective-permute-start.22 = (bf16[2,256,1024]{2,1,0:T(8,128)(2,1)}, bf16[2,256,1024]{2,1,0:T(8,128)(2,1)S(1)}, u32[]{:S(2)}, u32[]{:S(2)}) collective-permute-start(bf16[2,256,1024]{2,1,0:T(8,128)(2,1)} %get-tuple-element.116), channel_id=1, source_target_pairs={{0,1},{1,0},{2,3},{3,2},{4,5},{5,4},{6,7},{7,6},{8,9},{9,8},{10,11... | collective-permute-start | bytes 3145736 | tf_op jit(solution)/shard_map/ppermute | solution.py:68
  150.5 158.6 %reduce-scatter.13.cloned.1.call-start = ((), (), s32[]{:S(2)}) async-start(), calls=%async_computation.5 | async-start | bytes 589824
  150.8 13.9 %collective-permute-start.23 = (bf16[1,256,1024]{2,1,0:T(8,128)(2,1)S(1)}, bf16[1,256,1024]{2,1,0:T(8,128)(2,1)S(1)}, u32[]{:S(2)}, u32[]{:S(2)}) collective-permute-start(bf16[1,256,1024]{2,1,0:T(8,128)(2,1)S(1)} %slice_add_fusion), channel_id=1, source_target_pairs={{0,2},{1,3},{2,0},{3,1},{4,6},{5,7},{6,4},{7,5},{8,10},{9,11},{10,... | collective-permute-start | bytes 1572872 | tf_op jit(solution)/shard_map/ppermute | solution.py:68
  168.7 13.4 %collective-permute-start.25 = (bf16[256,1024]{1,0:T(8,128)(2,1)}, bf16[256,1024]{1,0:T(8,128)(2,1)S(1)}, u32[]{:S(2)}, u32[]{:S(2)}) collective-permute-start(bf16[256,1024]{1,0:T(8,128)(2,1)} %get-tuple-element.121.refs_0_), channel_id=1, source_target_pairs={{0,2},{1,3},{2,0},{3,1},{4,6},{5,7},{6,4},{7,5},{8,10},{9,11},{10,... | collective-permute-start | bytes 1572872 | tf_op jit(solution)/shard_map/ppermute | solution.py:68
  170.2 11.9 %collective-permute-start.24 = (bf16[256,1024]{1,0:T(8,128)(2,1)}, bf16[256,1024]{1,0:T(8,128)(2,1)S(1)}, u32[]{:S(2)}, u32[]{:S(2)}) collective-permute-start(bf16[256,1024]{1,0:T(8,128)(2,1)} %get-tuple-element.121.refs_0_), channel_id=1, source_target_pairs={{0,1},{1,0},{2,3},{3,2},{4,5},{5,4},{6,7},{7,6},{8,9},{9,8},{10,11... | collective-permute-start | bytes 1572872 | tf_op jit(solution)/shard_map/ppermute | solution.py:68
  182.1 1.9 collective-permute-start.26
  194.6 159.7 %reduce-scatter.15.cloned.1.call-start = ((), (), s32[]{:S(2)}) async-start(), calls=%async_computation.6 | async-start | bytes 3244032
  212.5 209.8 %reduce-scatter.11.cloned.1.call-start = ((), (), s32[]{:S(2)}) async-start(), calls=%async_computation.4 | async-start | bytes 1769472 | tf_op jit(solution)/shard_map/reduce_scatter | solution.py:1176
  213.4 8.3 %collective-permute-start.27 = (bf16[528,128]{1,0:T(8,128)(2,1)S(1)}, bf16[528,128]{1,0:T(8,128)(2,1)S(1)}, u32[]{:S(2)}, u32[]{:S(2)}) collective-permute-start(bf16[528,128]{1,0:T(8,128)(2,1)S(1)} %copy-done.32), channel_id=1, source_target_pairs={{8,0},{12,4},{16,8},{20,12},{24,16},{28,20},{9,1},{13,5},{17,9},{2... | collective-permute-start | bytes 405512 | tf_op jit(solution)/shard_map/ppermute | solution.py:73
  214.7 7.5 %collective-permute-start.28 = (bf16[528,128]{1,0:T(8,128)(2,1)S(1)}, bf16[528,128]{1,0:T(8,128)(2,1)S(1)}, u32[]{:S(2)}, u32[]{:S(2)}) collective-permute-start(bf16[528,128]{1,0:T(8,128)(2,1)S(1)} %copy-done.32), channel_id=1, source_target_pairs={{4,0},{8,4},{12,8},{16,12},{20,16},{24,20},{28,24},{5,1},{9,5},{13... | collective-permute-start | bytes 405512 | tf_op jit(solution)/shard_map/ppermute | solution.py:73
  224.8 8.5 %collective-permute-start.29 = (bf16[528,128]{1,0:T(8,128)(2,1)}, bf16[528,128]{1,0:T(8,128)(2,1)S(1)}, u32[]{:S(2)}, u32[]{:S(2)}) collective-permute-start(bf16[528,128]{1,0:T(8,128)(2,1)} %get-tuple-element.145), channel_id=1, source_target_pairs={{8,0},{12,4},{16,8},{20,12},{24,16},{28,20},{9,1},{13,5},{17,9},{2... | collective-permute-start | bytes 405512 | tf_op jit(solution)/shard_map/ppermute | solution.py:73
  235.8 11.6 %collective-permute-start.30 = (bf16[528,128]{1,0:T(8,128)(2,1)}, bf16[528,128]{1,0:T(8,128)(2,1)S(1)}, u32[]{:S(2)}, u32[]{:S(2)}) collective-permute-start(bf16[528,128]{1,0:T(8,128)(2,1)} %get-tuple-element.147), channel_id=1, source_target_pairs={{16,0},{20,4},{24,8},{28,12},{17,1},{21,5},{25,9},{29,13},{18,2},{... | collective-permute-start | bytes 405512 | tf_op jit(solution)/shard_map/ppermute | solution.py:73
  249.9 17.7 %copy-start.37 = (bf16[1024,1024]{1,0:T(8,128)(2,1)S(1)}, bf16[1024,1024]{1,0:T(8,128)(2,1)}, u32[]{:S(2)}) copy-start(bf16[1024,1024]{1,0:T(8,128)(2,1)} %get-tuple-element.165) | copy-start | bytes 6291460
  259.9 6.3 %collective-permute-start.31 = (f32[8,768]{1,0:T(8,128)}, f32[8,768]{1,0:T(8,128)S(1)}, u32[]{:S(2)}, u32[]{:S(2)}) collective-permute-start(f32[8,768]{1,0:T(8,128)} %get-tuple-element.154), channel_id=1, source_target_pairs={{4,0},{8,4},{12,8},{16,12},{20,16},{24,20},{28,24},{5,1},{9,5},{13... | collective-permute-start | bytes 73736 | tf_op jit(solution)/shard_map/ppermute | solution.py:73
  272.4 16.9 %collective-permute-start.20 = (bf16[2,1024,256]{2,1,0:T(8,128)(2,1)}, bf16[2,1024,256]{2,1,0:T(8,128)(2,1)S(1)}, u32[]{:S(2)}, u32[]{:S(2)}) collective-permute-start(bf16[2,1024,256]{2,1,0:T(8,128)(2,1)} %get-tuple-element.110), channel_id=1, source_target_pairs={{0,1},{1,0},{2,3},{3,2},{4,5},{5,4},{6,7},{7,6},{8,9},{9,8},{10,11... | collective-permute-start | bytes 3145736 | tf_op jit(solution)/shard_map/ppermute | solution.py:68
  273.2 16.1 %copy-start.4 = (bf16[1024,256]{1,0:T(8,128)(2,1)S(1)}, bf16[1024,256]{1,0:T(8,128)(2,1)}, u32[]{:S(2)}) copy-start(bf16[1024,256]{1,0:T(8,128)(2,1)} %get-tuple-element.111) | copy-start | bytes 1572868
  280.3 18.7 %copy-start.5 = (bf16[1024,256]{1,0:T(8,128)(2,1)S(1)}, bf16[1024,256]{1,0:T(8,128)(2,1)}, u32[]{:S(2)}) copy-start(bf16[1024,256]{1,0:T(8,128)(2,1)} %get-tuple-element.158) | copy-start | bytes 1572868
  281.1 1.4 collective-permute-start.34
  281.7 17.3 %collective-permute-start.32 = (bf16[2,1024,256]{2,1,0:T(8,128)(2,1)}, bf16[2,1024,256]{2,1,0:T(8,128)(2,1)S(1)}, u32[]{:S(2)}, u32[]{:S(2)}) collective-permute-start(bf16[2,1024,256]{2,1,0:T(8,128)(2,1)} %get-tuple-element.157), channel_id=1, source_target_pairs={{0,1},{1,0},{2,3},{3,2},{4,5},{5,4},{6,7},{7,6},{8,9},{9,8},{10,11... | collective-permute-start | bytes 3145736 | tf_op jit(solution)/shard_map/ppermute | solution.py:68
  282.5 3.7 collective-permute-start.35
  286.2 6.1 %collective-permute-start.36 = (f32[46,256]{1,0:T(8,128)S(1)}, f32[46,256]{1,0:T(8,128)S(1)}, u32[]{:S(2)}, u32[]{:S(2)}) collective-permute-start(f32[46,256]{1,0:T(8,128)S(1)} %pad_maximum_fusion.2), channel_id=1, source_target_pairs={{0,4},{4,0},{8,12},{12,8},{16,20},{20,16},{24,28},{28,24},{1,5},{5... | collective-permute-start | bytes 141320 | tf_op jit(solution)/shard_map/ppermute | solution.py:68
  289.4 14.9 %collective-permute-start.21 = (bf16[1024,256]{1,0:T(8,128)(2,1)S(1)}, bf16[1024,256]{1,0:T(8,128)(2,1)S(1)}, u32[]{:S(2)}, u32[]{:S(2)}) collective-permute-start(bf16[1024,256]{1,0:T(8,128)(2,1)S(1)} %fusion.14), channel_id=1, source_target_pairs={{0,2},{1,3},{2,0},{3,1},{4,6},{5,7},{6,4},{7,5},{8,10},{9,11},{10,... | collective-permute-start | bytes 1572872 | tf_op jit(solution)/shard_map/ppermute | solution.py:68
  292.4 6.5 %collective-permute-start.37 = (f32[46,256]{1,0:T(8,128)S(1)}, f32[46,256]{1,0:T(8,128)S(1)}, u32[]{:S(2)}, u32[]{:S(2)}) collective-permute-start(f32[46,256]{1,0:T(8,128)S(1)} %fusion.26), channel_id=1, source_target_pairs={{0,8},{4,12},{8,0},{12,4},{16,24},{20,28},{24,16},{28,20},{1,9},{5... | collective-permute-start | bytes 141320 | tf_op jit(solution)/shard_map/ppermute | solution.py:68
  298.9 8.4 %collective-permute-start.38 = (f32[46,256]{1,0:T(8,128)S(1)}, f32[46,256]{1,0:T(8,128)S(1)}, u32[]{:S(2)}, u32[]{:S(2)}) collective-permute-start(f32[46,256]{1,0:T(8,128)S(1)} %add.70), channel_id=1, source_target_pairs={{0,16},{4,20},{8,24},{12,28},{16,0},{20,4},{24,8},{28,12},{1,17},{... | collective-permute-start | bytes 141320 | tf_op jit(solution)/shard_map/ppermute | solution.py:68
  299.1 14.5 %collective-permute-start.33 = (bf16[1024,256]{1,0:T(8,128)(2,1)S(1)}, bf16[1024,256]{1,0:T(8,128)(2,1)}, u32[]{:S(2)}, u32[]{:S(2)}) collective-permute-start(bf16[1024,256]{1,0:T(8,128)(2,1)S(1)} %fusion.13), channel_id=1, source_target_pairs={{0,2},{1,3},{2,0},{3,1},{4,6},{5,7},{6,4},{7,5},{8,10},{9,11},{10,... | collective-permute-start | bytes 1572872 | tf_op jit(solution)/shard_map/ppermute | solution.py:68
  (34 other events, 156.1 us)
Sparse Core Ops, SparseCore 0:
  150.6 62.0 reduce-scatter.16
  216.4 60.8 reduce-scatter.12
  280.8 73.4 reduce-scatter.14
  357.6 64.6 reduce-scatter.10
